TPU v7x, 32 devices: a whole 2x2x4 slice. The times are simulated.
32 devices in a mesh: dom: 8 (over z, x), local: 4 (over y, core).
Axes of the slice: x: 2, y: 2, z: 4, core: 2. Of those that a mesh axis runs over, the one named last changes fastest.
Arguments:
- features: bfloat16 [65536, 128], P(('dom', 'local')), may hold values from -6 to 6
- serve_rows: int32 [256, 4], P(('dom', 'local')), may hold values from 0 to 2047
- pick_rows: int32 [128, 128], P(('dom', 'local')), may hold values from 0 to 31
- neighbours: int32 [32768, 15], P(('dom', 'local')), may hold values from 0 to 511
- batch_nodes: int32 [32768], P(('dom', 'local')), may hold values from 0 to 2047
- w_self: bfloat16 [128, 256], replicated, may hold values from -0.5 to 0.5
- w_neigh: bfloat16 [128, 256], replicated, may hold values from -1 to 1
- cotangent: bfloat16 [32768, 256], P(('dom', 'local')), may hold values from -6 to 6
Outputs:
- hidden: bfloat16 [32768, 256], P(('dom', 'local'))
- grad_self: float32 [128, 256], replicated
- grad_neigh: float32 [128, 256], replicated
All inputs are finite; a program needn't handle non-finite values.
Results may differ from a plain program's by a relative error of at most 0.0051.
Values may be sent and summed in bfloat16 or wider, within the bound.
No kernel may reach another device: no remote copies, remote signals or barrier semaphores. Data moves between devices by JAX's collectives and lax.ppermute only.
A program may use at most 64 MiB of HBM per device.

v0:
```python
import math

import jax
import jax.numpy as jnp
from jax import lax
from jax.sharding import PartitionSpec as P


def local(features, serve_rows, pick_rows, neighbours, batch_nodes, w_self, w_neigh, cotangent):
    n_dom = lax.axis_size("dom")
    n_local = lax.axis_size("local")
    width = features.shape[1]
    outgoing = jnp.take(features, serve_rows, axis=0)
    arrived = lax.all_to_all(outgoing, "dom", split_axis=0, concat_axis=0, tiled=True)
    collected = arrived.reshape(-1, width)
    wanted = lax.all_to_all(pick_rows, "local", split_axis=0, concat_axis=0, tiled=True)
    taken = jnp.take(collected, wanted, axis=0)
    pool = lax.all_to_all(taken, "local", split_axis=0, concat_axis=0, tiled=True).reshape(
        -1, width
    )
    rows = jnp.take(pool, neighbours, axis=0)
    neighbour_mean = (jnp.sum(rows.astype(jnp.float32), axis=1) / neighbours.shape[1]).astype(
        jnp.bfloat16
    )
    self_rows = jnp.take(features, batch_nodes, axis=0)
    pre = jnp.dot(self_rows, w_self, preferred_element_type=jnp.float32) + jnp.dot(
        neighbour_mean, w_neigh, preferred_element_type=jnp.float32
    )
    sigma = jax.nn.sigmoid(pre)
    hidden = (pre * sigma).astype(jnp.bfloat16)
    slope = (cotangent.astype(jnp.float32) * sigma * (1.0 + pre * (1.0 - sigma))).astype(
        jnp.bfloat16
    )
    scale = 1.0 / math.sqrt(n_dom * n_local * batch_nodes.shape[0])
    contract = (((0,), (0,)), ((), ()))
    term_self = (
        lax.dot_general(self_rows, slope, contract, preferred_element_type=jnp.float32) * scale
    )
    term_neigh = (
        lax.dot_general(neighbour_mean, slope, contract, preferred_element_type=jnp.float32) * scale
    )
    terms = jnp.stack([term_self, term_neigh])
    summed = lax.psum(terms, ("dom", "local"))
    return (hidden, summed[0], summed[1])


def solution(mesh):
    placed = (
        P(("dom", "local"), None),
        P(("dom", "local"), None),
        P(("dom", "local"), None),
        P(("dom", "local"), None),
        P(("dom", "local")),
        P(),
        P(),
        P(("dom", "local"), None),
    )
    return jax.shard_map(
        local,
        mesh=mesh,
        in_specs=placed,
        out_specs=(P(("dom", "local"), None), P(), P()),
        check_vma=False,
    )
```

profile of v0, /device:TPU:0, one launch (start us, length us, event | category | flops | bytes accessed | tf_op | source)
XLA Modules:
  0.0 251.4 jit_solution(18054839927957434187)
XLA Ops:
  7.2 4.4 %all-to-all-start = ((s32[4,1,128]{2,1,0:T(1,128)}), s32[4,1,128]{2,1,0:T(1,128)S(1)}, u32[]{:S(2)}, u32[]{:S(2)}) async-start(s32[4,1,128]{2,1,0:T(1,128)} %bitcast.27), calls=%async_computation | async-start | bytes 4096 | tf_op jit(solution)/shard_map/all_to_all | solution.py:16
  11.6 0.7 compare_select_fusion.3
  12.3 0.7 compare_and_fusion.2
  12.9 0.7 fusion.3
  13.6 0.7 compare_and_fusion.1
  14.3 0.1 copy.20
  14.4 0.1 reshape.75
  14.5 0.1 copy.19
  14.6 0.9 compare_select_fusion
  15.4 0.2 copy.21
  15.7 0.3 reshape.91
  16.0 0.6 gather_fusion.1
  16.6 3.2 %gather_fusion = bf16[1024,128]{1,0:T(8,128)(2,1)S(1)} fusion(bf16[2048,128]{1,0:T(8,128)(2,1)S(1)} %copy-done, s32[1024]{0:T(1024)S(1)} %fusion.3), kind=kCustom, calls=%fused_computation | custom fusion | bytes 528384 | tf_op jit(solution)/shard_map/jit(_take)/gather | solution.py:25
  19.8 1.2 fusion.2
  21.0 0.7 broadcast_select_fusion.4
  21.7 6.2 %all-to-all-start.1 = ((bf16[8,4,128]{2,1,0:T(4,128)(2,1)}), bf16[8,4,128]{2,1,0:T(4,128)(2,1)S(1)}, u32[]{:S(2)}, u32[]{:S(2)}) async-start(bf16[8,4,128]{2,1,0:T(4,128)(2,1)} %broadcast_select_fusion.4), calls=%async_computation.1 | async-start | bytes 16384 | tf_op jit(solution)/shard_map/all_to_all | solution.py:14
  28.0 6.5 %all-to-all-done.1 = bf16[8,4,128]{2,1,0:T(4,128)(2,1)S(1)} async-done(((bf16[8,4,128]{2,1,0:T(4,128)(2,1)}), bf16[8,4,128]{2,1,0:T(4,128)(2,1)S(1)}, u32[]{:S(2)}, u32[]{:S(2)}) %all-to-all-start.1) | async-done | bytes 8224 | tf_op jit(solution)/shard_map/all_to_all | solution.py:14
  34.5 1.3 gather_fusion.2
  35.8 0.8 broadcast_select_fusion.1
  36.6 3.3 %all-to-all-start.2 = ((bf16[4,128,128]{2,1,0:T(8,128)(2,1)}), bf16[4,128,128]{2,1,0:T(8,128)(2,1)S(1)}, u32[]{:S(2)}, u32[]{:S(2)}) async-start(bf16[4,128,128]{2,1,0:T(8,128)(2,1)} %broadcast_select_fusion.1), calls=%async_computation.2 | async-start | bytes 262144 | tf_op jit(solution)/shard_map/all_to_all | solution.py:18
  40.0 0.0 all-reduce.2.cloned.1.call-start
  40.0 0.3 copy.18
  40.3 4.2 %all-to-all-done.2 = bf16[4,128,128]{2,1,0:T(8,128)(2,1)S(1)} async-done(((bf16[4,128,128]{2,1,0:T(8,128)(2,1)}), bf16[4,128,128]{2,1,0:T(8,128)(2,1)S(1)}, u32[]{:S(2)}, u32[]{:S(2)}) %all-to-all-start.2) | async-done | bytes 131104 | tf_op jit(solution)/shard_map/all_to_all | solution.py:18
  44.5 54.0 %gather_fusion.3 = bf16[15360,128]{1,0:T(8,128)(2,1)} fusion(bf16[512,128]{1,0:T(8,128)(2,1)S(1)} %bitcast.21, s32[15360]{0:T(1024)S(1)} %broadcast_clamp_fusion), kind=kCustom, calls=%fused_computation.3 | custom fusion | bytes 7925760 | tf_op jit(solution)/shard_map/jit(_take)/gather | solution.py:21
  98.5 6.9 %reshape.90 = bf16[1024,15,128]{2,1,0:T(8,128)(2,1)} reshape(bf16[15360,128]{1,0:T(8,128)(2,1)} %gather_fusion.3) | data formatting | bytes 7864320 | tf_op jit(solution)/shard_map/jit(_take)/gather | solution.py:21
  105.4 13.0 %convert_reduce_fusion = f32[1024,128]{1,0:T(8,128)S(1)} fusion(bf16[1024,15,128]{2,1,0:T(8,128)(2,1)} %reshape.90, pred[1024,15]{1,0:T(8,128)(4,1)S(1)} %copy.18), kind=kLoop, calls=%fused_computation.4 | loop fusion | flops 5767168 | bytes 4471808 | tf_op jit(solution)/shard_map/reduce_sum | solution.py:22
  118.5 1.5 multiply_convert_fusion
  119.9 0.3 fusion
  120.2 0.4 fusion.1
  120.6 0.7 pad_maximum_fusion
  121.4 121.5 %all-reduce.2.cloned.1.call-done = f32[2,128,256]{2,1,0:T(8,128)} async-done(((f32[2,128,256]{2,1,0:T(8,128)}), f32[2,128,256]{2,1,0:T(8,128)}) %all-reduce.2.cloned.1.call-update) | async-done | bytes 262160 | tf_op jit(solution)/shard_map/psum | solution.py:43
  242.9 1.7 slice_bitcast_fusion
  (16 shorter events, 0.1 us)
Async XLA Ops:
  7.2 8.9 %copy-start = (bf16[2048,128]{1,0:T(8,128)(2,1)S(1)}, bf16[2048,128]{1,0:T(8,128)(2,1)}, u32[]{:S(2)}) copy-start(bf16[2048,128]{1,0:T(8,128)(2,1)} %param.8) | copy-start | bytes 1572868
  7.2 32.8 %copy-start.1 = (s32[1024,15]{0,1:T(8,128)S(1)}, s32[1024,15]{0,1:T(8,128)}, u32[]{:S(2)}) copy-start(s32[1024,15]{0,1:T(8,128)} %param.11) | copy-start | bytes 184324
  7.2 14.5 %all-to-all-start = ((s32[4,1,128]{2,1,0:T(1,128)}), s32[4,1,128]{2,1,0:T(1,128)S(1)}, u32[]{:S(2)}, u32[]{:S(2)}) async-start(s32[4,1,128]{2,1,0:T(1,128)} %bitcast.27), calls=%async_computation | async-start | bytes 4096 | tf_op jit(solution)/shard_map/all_to_all | solution.py:16
  21.7 12.8 %all-to-all-start.1 = ((bf16[8,4,128]{2,1,0:T(4,128)(2,1)}), bf16[8,4,128]{2,1,0:T(4,128)(2,1)S(1)}, u32[]{:S(2)}, u32[]{:S(2)}) async-start(bf16[8,4,128]{2,1,0:T(4,128)(2,1)} %broadcast_select_fusion.4), calls=%async_computation.1 | async-start | bytes 16384 | tf_op jit(solution)/shard_map/all_to_all | solution.py:14
  36.6 7.9 %all-to-all-start.2 = ((bf16[4,128,128]{2,1,0:T(8,128)(2,1)}), bf16[4,128,128]{2,1,0:T(8,128)(2,1)S(1)}, u32[]{:S(2)}, u32[]{:S(2)}) async-start(bf16[4,128,128]{2,1,0:T(8,128)(2,1)} %broadcast_select_fusion.1), calls=%async_computation.2 | async-start | bytes 262144 | tf_op jit(solution)/shard_map/all_to_all | solution.py:18
  40.0 203.0 %all-reduce.2.cloned.1.call-start = ((), (), s32[]{:S(2)}) async-start(), calls=%async_computation.3 | async-start | bytes 524288 | tf_op jit(solution)/shard_map/psum | solution.py:43
  105.4 13.0 %copy-start.2 = (bf16[1024,256]{1,0:T(8,128)(2,1)S(1)}, bf16[1024,256]{1,0:T(8,128)(2,1)}, u32[]{:S(2)}) copy-start(bf16[1024,256]{1,0:T(8,128)(2,1)} %param.15) | copy-start | bytes 1572868
  105.4 13.0 %copy-start.3 = (bf16[128,256]{1,0:T(8,128)(2,1)S(1)}, bf16[128,256]{1,0:T(8,128)(2,1)}, u32[]{:S(2)}) copy-start(bf16[128,256]{1,0:T(8,128)(2,1)} %param.14) | copy-start | bytes 196612
Sparse Core Ops, SparseCore 0:
  121.5 121.3 all-reduce.1
where the time goes:
time: 252 us; the launch traced here: 251 us
  waiting for transfers between devices  132 us (52%)
  local copies, waits for them, and re-layouts  68.8 us (27%)
  other arithmetic  18.9 us (7%)
  between operations  14.2 us (6%)
  starting transfers between devices  14 us (6%)
  matrix products  3.36 us (1%)
    psum x1, waiting for transfers between devices, local(): summed = lax.psum(terms, ('dom', 'local'))  122 us
    gather x2, local copies, waits for them, and re-layouts, local(): rows = jnp.take(pool, neighbours, axis=0)  60.9 us
    reduce_sum x1, other arithmetic, local(): jnp.sum(rows.astype(jnp.float32), axis=1) / neighbours.shape[1]  13 us
    all_to_all x1, waiting for transfers between devices, local(): lax.all_to_all(outgoing, 'dom', split_axis=0, concat_axis=0, tiled=True)  6.48 us
    all_to_all x1, starting transfers between devices, local(): lax.all_to_all(outgoing, 'dom', split_axis=0, concat_axis=0, tiled=True)  6.24 us
  transfers between devices with their start and end apart: 4, of which 3 were waited for; matrix products, arithmetic and copies ran while one was open for 4% of the time, Pallas kernels for 0%

commit v1 on v0

v1 whole, which is shorter than its diff:
```python
import functools
import math

import jax
import jax.numpy as jnp
from jax import lax
from jax.experimental import pallas as pl
from jax.experimental.pallas import tpu as pltpu
from jax.sharding import PartitionSpec as P

AXES = ("dom", "local")
LANES = 128
VMEM = pl.BlockSpec(memory_space=pltpu.VMEM)


def call(kernel, out_shape, operands, flops, bytes_accessed, scratch=()):
    return pl.pallas_call(
        kernel,
        out_shape=out_shape,
        in_specs=[VMEM] * len(operands),
        out_specs=jax.tree.map(lambda _: VMEM, out_shape),
        scratch_shapes=list(scratch),
        compiler_params=pltpu.CompilerParams(vmem_limit_bytes=40 * 2**20),
        cost_estimate=pl.CostEstimate(
            flops=flops, bytes_accessed=bytes_accessed, transcendentals=0
        ),
    )(*operands)


def serve_kernel(n_local, serve_ref, features_ref, out_ref):
    cap, n_dom = serve_ref.shape
    n_nodes = features_ref.shape[0]
    serve = serve_ref[...].astype(jnp.float32)
    block = 128
    for base in range(0, out_ref.shape[0], block):
        row = base + lax.broadcasted_iota(jnp.int32, (block, n_dom), 0)
        wanted = jnp.zeros((block, n_dom), jnp.float32)
        for c in range(cap):
            wanted = jnp.where(row % cap == c, serve[c : c + 1, :], wanted)
        group = lax.broadcasted_iota(jnp.int32, (block, n_dom), 1)
        mine = group == row // (cap * n_local)
        index = jnp.sum(jnp.where(mine, wanted, 0.0), axis=1, keepdims=True).astype(jnp.int32)
        node = lax.broadcasted_iota(jnp.int32, (block, n_nodes), 1)
        chosen = jnp.where(node == index, 1.0, 0.0).astype(jnp.bfloat16)
        out_ref[base : base + block, :] = jnp.dot(
            chosen, features_ref[...], preferred_element_type=jnp.float32
        ).astype(jnp.bfloat16)


def local_kernel(
    n_local, cap, pick_ref, neighbours_ref, nodes_ref, features_ref, self_ref, counts_ref
):
    n_rows = counts_ref.shape[1]
    n_nodes = features_ref.shape[0]
    fanout, batch = neighbours_ref.shape
    pick = pick_ref[...]
    source = lax.broadcasted_iota(jnp.int32, pick.shape, 0)
    place = (pick // cap) * (n_local * cap) + source * cap + pick % cap
    nodes = nodes_ref[...].T
    for j in range(batch // LANES):
        rows = slice(j * LANES, (j + 1) * LANES)
        near = neighbours_ref[:, rows]
        lane, tile = near % LANES, near // LANES
        where = jnp.zeros_like(near)
        for m in range(pick.shape[0]):
            table = jnp.broadcast_to(place[m : m + 1, :], near.shape)
            found = jnp.take_along_axis(table, lane, axis=1)
            where = jnp.where(tile == m, found, where)
        for base in range(0, n_rows, LANES):
            row = base + lax.broadcasted_iota(jnp.int32, (LANES, LANES), 0)
            count = jnp.zeros((LANES, LANES), jnp.float32)
            for k in range(fanout):
                count += jnp.where(where[k : k + 1, :] == row, 1.0, 0.0)
            counts_ref[rows, base : base + LANES] = count.T.astype(jnp.bfloat16)
        node = lax.broadcasted_iota(jnp.int32, (LANES, n_nodes), 1)
        chosen = jnp.where(node == nodes[:, j : j + 1], 1.0, 0.0).astype(jnp.bfloat16)
        self_ref[rows, :] = jnp.dot(
            chosen, features_ref[...], preferred_element_type=jnp.float32
        ).astype(jnp.bfloat16)


def layer_kernel(
    fanout,
    scale,
    arrived_ref,
    counts_ref,
    self_ref,
    w_self_ref,
    w_neigh_ref,
    cotangent_ref,
    hidden_ref,
    partial_ref,
    inputs_ref,
    slope_ref,
    weights_ref,
):
    width = self_ref.shape[1]
    batch, units = cotangent_ref.shape
    weights_ref[:width, :] = w_self_ref[...]
    weights_ref[width:, :] = w_neigh_ref[...]
    step = 256
    for base in range(0, batch, step):
        rows = slice(base, base + step)
        inputs_ref[rows, :width] = self_ref[rows, :]
        total = jnp.dot(counts_ref[rows, :], arrived_ref[...], preferred_element_type=jnp.float32)
        inputs_ref[rows, width:] = (total * (1.0 / fanout)).astype(jnp.bfloat16)
        pre = jnp.dot(inputs_ref[rows, :], weights_ref[...], preferred_element_type=jnp.float32)
        sigma = jax.nn.sigmoid(pre)
        hidden_ref[rows, :] = (pre * sigma).astype(jnp.bfloat16)
        slope_ref[rows, :] = (
            cotangent_ref[rows, :].astype(jnp.float32) * sigma * (1.0 + pre * (1.0 - sigma))
        ).astype(jnp.bfloat16)
    terms = lax.dot_general(
        inputs_ref[...],
        slope_ref[...],
        (((0,), (0,)), ((), ())),
        preferred_element_type=jnp.float32,
    )
    terms = (terms * scale).astype(jnp.bfloat16)
    for i in range(units // LANES):
        partial_ref[i * 2 * width : (i + 1) * 2 * width, :] = terms[:, i * LANES : (i + 1) * LANES]


def unpack_kernel(packed_ref, grad_self_ref, grad_neigh_ref):
    width, units = grad_self_ref.shape
    for i in range(units // LANES):
        columns = slice(i * LANES, (i + 1) * LANES)
        base = i * 2 * width
        grad_self_ref[:, columns] = packed_ref[base : base + width, :].astype(jnp.float32)
        grad_neigh_ref[:, columns] = packed_ref[base + width : base + 2 * width, :].astype(
            jnp.float32
        )


def local(features, serve_rows, pick_rows, neighbours, batch_nodes, w_self, w_neigh, cotangent):
    n_dom = lax.axis_size("dom")
    n_local = lax.axis_size("local")
    n_devices = n_dom * n_local
    n_nodes, width = features.shape
    batch, fanout = neighbours.shape
    units = w_self.shape[1]
    cap = serve_rows.shape[1]
    n_rows = n_devices * cap
    bf16, f32 = jnp.bfloat16, jnp.float32
    struct = jax.ShapeDtypeStruct

    outgoing = call(
        functools.partial(serve_kernel, n_local),
        struct((n_rows, width), bf16),
        (serve_rows.T, features),
        2 * n_rows * n_nodes * width,
        2 * n_nodes * width,
    )
    arrived = lax.all_to_all(
        outgoing.reshape(n_devices, cap, width), AXES, split_axis=0, concat_axis=0, tiled=True
    ).reshape(n_rows, width)
    self_rows, counts = call(
        functools.partial(local_kernel, n_local, cap),
        (struct((batch, width), bf16), struct((batch, n_rows), bf16)),
        (pick_rows, neighbours.T, batch_nodes.reshape(-1, LANES), features),
        2 * batch * n_nodes * width,
        2 * n_nodes * width,
    )
    scale = 1.0 / math.sqrt(n_devices * batch)
    hidden, partial = call(
        functools.partial(layer_kernel, fanout, scale),
        (struct((batch, units), bf16), struct((2 * width * units // LANES, LANES), bf16)),
        (arrived, counts, self_rows, w_self, w_neigh, cotangent),
        8 * batch * width * units,
        4 * batch * units,
        (
            pltpu.VMEM((batch, 2 * width), bf16),
            pltpu.VMEM((batch, units), bf16),
            pltpu.VMEM((2 * width, units), bf16),
        ),
    )
    packed = partial.shape[0]
    share = -(-packed // n_devices)
    if share * n_devices != packed:
        partial = jnp.pad(partial, ((0, share * n_devices - packed), (0, 0)))
    pieces = lax.all_to_all(
        partial.reshape(n_devices, share, LANES), AXES, split_axis=0, concat_axis=0, tiled=True
    )
    summed = jnp.sum(pieces.astype(f32), axis=0).astype(bf16)
    gathered = lax.all_to_all(
        jnp.broadcast_to(summed, pieces.shape), AXES, split_axis=0, concat_axis=0, tiled=True
    ).reshape(n_devices * share, LANES)
    grad_self, grad_neigh = call(
        unpack_kernel,
        (struct((width, units), f32), struct((width, units), f32)),
        (gathered,),
        0,
        12 * width * units,
    )
    return hidden, grad_self, grad_neigh


def solution(mesh):
    rows = P(AXES, None)
    return jax.shard_map(
        local,
        mesh=mesh,
        in_specs=(rows, rows, rows, rows, P(AXES), P(), P(), rows),
        out_specs=(rows, P(), P()),
        check_vma=False,
    )
```

time: 252 us -> 40.5 us (0.16)
  waiting for transfers between devices: 132 us -> 4.71 us
  local copies, waits for them, and re-layouts: 68.8 us -> 1.77 us
  blocking collectives: 0 us -> 19.8 us
  other arithmetic: 18.9 us -> 0.04 us
  between operations: 14.2 us -> 0.73 us
  starting transfers between devices: 14 us -> 7.3 us
  Pallas kernels: 0 us -> 5.83 us
  matrix products: 3.36 us -> 0 us
    psum x1 -> x0, waiting for transfers between devices: 122 us -> none  [local(): summed = lax.psum(terms, ('dom', 'local'))]
    gather x5 -> x0, local copies, waits for them, and re-layouts: 66 us -> none  [the longest x2 60.9 us: local(): rows = jnp.take(pool, neighbours, axis=0)]
    all_to_all x0 -> x2, blocking collectives: none -> 19.8 us  [the longest x1 9.93 us: local(): lax.all_to_all(jnp.broadcast_to(summed, pieces.shape), AXES, split_axis=0...]
    reduce_sum x1, other arithmetic: 13 us -> 0.04 us  [local(): summed = jnp.sum(pieces.astype(f32), axis=0).astype(bf16)]
    all_to_all x3 -> x1, starting transfers between devices: 13.9 us -> 7.3 us  [local(): lax.all_to_all(outgoing.reshape(n_devices, cap, width), AXES, split_axis=...]
    all_to_all x3 -> x1, waiting for transfers between devices: 10.7 us -> 4.71 us  [local(): lax.all_to_all(outgoing.reshape(n_devices, cap, width), AXES, split_axis=...]
    pallas_call x0 -> x4, Pallas kernels: none -> 5.83 us  [call(): pl.pallas_call(kernel, out_shape=out_shape, in_specs=[VMEM] * len(operand...]
    dot_general x4 -> x0, matrix products: 3.36 us -> none  [the longest x1 1.47 us: local(): jnp.dot(neighbour_mean, w_neigh, preferred_element_type=jnp.float32)]
  transfers between devices with their start and end apart: 4 -> 1, of which waited for: 3 -> 1; matrix products, arithmetic and copies ran while one was open for 4% -> 0% of each run, Pallas kernels for 0% -> 6%
where the time goes in v1:
time: 40.5 us; the launch traced here: 40.2 us
  blocking collectives  19.8 us (49%)
  starting transfers between devices  7.3 us (18%)
  Pallas kernels  5.83 us (14%)
  waiting for transfers between devices  4.71 us (12%)
  local copies, waits for them, and re-layouts  1.77 us (4%)
  between operations  0.73 us (2%)
    all_to_all x1, blocking collectives, local(): lax.all_to_all(jnp.broadcast_to(summed, pieces.shape), AXES, split_axis=0...  9.93 us
    all_to_all x1, blocking collectives, local(): lax.all_to_all(partial.reshape(n_devices, share, LANES), AXES, split_axis...  9.92 us
    all_to_all x1, starting transfers between devices, local(): lax.all_to_all(outgoing.reshape(n_devices, cap, width), AXES, split_axis=...  7.3 us
    pallas_call x4, Pallas kernels, call(): pl.pallas_call(kernel, out_shape=out_shape, in_specs=[VMEM] * len(operand...  5.83 us
    all_to_all x1, waiting for transfers between devices, local(): lax.all_to_all(outgoing.reshape(n_devices, cap, width), AXES, split_axis=...  4.71 us
    unnamed x18, local copies, waits for them, and re-layouts  1.75 us
  transfers between devices with their start and end apart: 1, of which 1 were waited for; matrix products, arithmetic and copies ran while one was open for 0% of the time, Pallas kernels for 6%

profile of v1, /device:TPU:0, one launch (start us, length us, event | category | flops | bytes accessed | tf_op | source)
XLA Modules:
  0.0 40.2 jit_solution(11973689632112074809)
XLA Ops:
  0.6 0.0 copy-start.1
  0.6 1.0 %copy-done.1 = bf16[2048,128]{1,0:T(8,128)(2,1)S(1)} copy-done((bf16[2048,128]{1,0:T(8,128)(2,1)S(1)}, bf16[2048,128]{1,0:T(8,128)(2,1)}, u32[]{:S(2)}) %copy-start.1) | copy-done | bytes 524312
  1.7 0.0 copy-start.5
  1.7 0.7 %copy-done.5 = s32[8,4]{0,1:T(4,128)S(1)} copy-done((s32[8,4]{0,1:T(4,128)S(1)}, s32[8,4]{0,1:T(4,128)}, u32[]{:S(2)}) %copy-start.5) | copy-done | bytes 152
  2.4 0.0 copy-start.2
  2.4 0.0 copy-start.8
  2.4 1.0 %shard_map.103 = bf16[128,128]{1,0:T(8,128)(2,1)} custom-call(s32[4,8]{1,0:T(4,128)S(1)} %bitcast.10, bf16[2048,128]{1,0:T(8,128)(2,1)S(1)} %copy-done.1), custom_call_target="tpu_custom_call" | custom-call | flops 67108864 | bytes 524288 | tf_op jit(solution)/shard_map/pallas_call | solution.py:17
  3.4 0.0 copy-start.6
  3.4 0.0 copy-start.7
  3.4 7.3 %all-to-all-start = ((bf16[32,4,128]{2,1,0:T(4,128)(2,1)}), bf16[32,4,128]{2,1,0:T(4,128)(2,1)S(1)}, u32[]{:S(2)}, u32[]{:S(2)}) async-start(bf16[32,4,128]{2,1,0:T(4,128)(2,1)} %bitcast.1), calls=%async_computation | async-start | bytes 65536 | tf_op jit(solution)/shard_map/all_to_all | solution.py:154
  10.7 0.0 copy-done.2
  10.7 0.0 copy-done.8
  10.7 0.0 copy-done.6
  10.7 0.0 copy-done.7
  10.7 0.0 copy-start
  10.7 0.0 copy-start.3
  10.8 0.0 copy-start.4
  10.8 2.5 %shard_map.104 = (bf16[1024,128]{1,0:T(8,128)(2,1)S(1)}, bf16[1024,128]{1,0:T(8,128)(2,1)S(1)}) custom-call(s32[4,128]{1,0:T(4,128)S(1)} %copy-done.8, s32[15,1024]{1,0:T(8,128)S(1)} %bitcast.11, s32[8,128]{1,0:T(8,128)S(1)} %bitcast.12, bf16[2048,128]{1,0:T(8,128)(2,1)S(1)} %copy-done.2), custom_call_target="tpu_custom_call" | custom-call | flops 536870912 | bytes 524288 | tf_op jit(solution)/shard_map/pallas_call | solution.py:17
  13.2 4.7 %all-to-all-done = bf16[32,4,128]{2,1,0:T(4,128)(2,1)S(1)} async-done(((bf16[32,4,128]{2,1,0:T(4,128)(2,1)}), bf16[32,4,128]{2,1,0:T(4,128)(2,1)S(1)}, u32[]{:S(2)}, u32[]{:S(2)}) %all-to-all-start) | async-done | bytes 32800 | tf_op jit(solution)/shard_map/all_to_all | solution.py:154
  17.9 0.0 copy-done
  17.9 0.0 copy-done.3
  18.0 0.0 copy-done.4
  18.0 1.6 %shard_map.105 = (bf16[1024,256]{1,0:T(8,128)(2,1)}, bf16[512,128]{1,0:T(8,128)(2,1)S(1)}) custom-call(bf16[128,128]{1,0:T(8,128)(2,1)S(1)} %bitcast.8, bf16[1024,128]{1,0:T(8,128)(2,1)S(1)} %get-tuple-element.9.counts_ref, bf16[1024,128]{1,0:T(8,128)(2,1)S(1)} %get-tuple-element.10.self_ref, bf16[128,256]{1,0:T(8,128)(2,1)S(1)} %copy-done.3, ...), custom_call_target="tpu_custom_call" | custom-call | flops 268435456 | bytes 1048576 | tf_op jit(solution)/shard_map/pallas_call | solution.py:17
  19.6 9.9 %all_to_all.15 = bf16[32,16,128]{2,1,0:T(8,128)(2,1)S(1)} all-to-all(bf16[32,16,128]{2,1,0:T(8,128)(2,1)S(1)} %bitcast.9), channel_id=1, replica_groups=mesh['dom'=8,'local'=4] {'dom','local'}, dimensions={0} | all-to-all | bytes 262144 | tf_op jit(solution)/shard_map/all_to_all | solution.py:181
  29.6 9.9 %all_to_all.16 = bf16[32,16,128]{2,1,0:T(8,128)(2,1)S(1)} all-to-all(bf16[32,16,128]{2,1,0:T(8,128)(2,1)S(1)} %broadcast_in_dim.3), channel_id=1, replica_groups=mesh['dom'=8,'local'=4] {'dom','local'}, dimensions={0} | all-to-all | bytes 262144 | tf_op jit(solution)/shard_map/all_to_all | solution.py:185
  39.5 0.7 %shard_map.106 = (f32[128,256]{1,0:T(8,128)}, f32[128,256]{1,0:T(8,128)}) custom-call(bf16[512,128]{1,0:T(8,128)(2,1)S(1)} %bitcast.7), custom_call_target="tpu_custom_call" | custom-call | bytes 393216 | tf_op jit(solution)/shard_map/pallas_call | solution.py:17
  (2 shorter events, 0.1 us)
Async XLA Ops:
  0.6 1.0 %copy-start.1 = (bf16[2048,128]{1,0:T(8,128)(2,1)S(1)}, bf16[2048,128]{1,0:T(8,128)(2,1)}, u32[]{:S(2)}) copy-start(bf16[2048,128]{1,0:T(8,128)(2,1)} %features_ref.3) | copy-start | bytes 1572868
  1.7 0.7 %copy-start.5 = (s32[8,4]{0,1:T(4,128)S(1)}, s32[8,4]{0,1:T(4,128)}, u32[]{:S(2)}) copy-start(s32[8,4]{0,1:T(4,128)} %param.9) | copy-start | bytes 388
  2.4 8.3 %copy-start.2 = (bf16[2048,128]{1,0:T(8,128)(2,1)S(1)}, bf16[2048,128]{1,0:T(8,128)(2,1)}, u32[]{:S(2)}) copy-start(bf16[2048,128]{1,0:T(8,128)(2,1)} %features_ref.3) | copy-start | bytes 1572868
  2.4 8.3 %copy-start.8 = (s32[4,128]{1,0:T(4,128)S(1)}, s32[4,128]{1,0:T(4,128)}, u32[]{:S(2)}) copy-start(s32[4,128]{1,0:T(4,128)} %pick_ref.1) | copy-start | bytes 6148
  3.4 7.3 %copy-start.6 = (s32[1024,15]{0,1:T(8,128)S(1)}, s32[1024,15]{0,1:T(8,128)}, u32[]{:S(2)}) copy-start(s32[1024,15]{0,1:T(8,128)} %param.11) | copy-start | bytes 184324
  3.4 7.3 %copy-start.7 = (s32[1024]{0:T(1024)S(1)}, s32[1024]{0:T(1024)}, u32[]{:S(2)}) copy-start(s32[1024]{0:T(1024)} %param.12) | copy-start | bytes 12292
  3.4 14.6 %all-to-all-start = ((bf16[32,4,128]{2,1,0:T(4,128)(2,1)}), bf16[32,4,128]{2,1,0:T(4,128)(2,1)S(1)}, u32[]{:S(2)}, u32[]{:S(2)}) async-start(bf16[32,4,128]{2,1,0:T(4,128)(2,1)} %bitcast.1), calls=%async_computation | async-start | bytes 65536 | tf_op jit(solution)/shard_map/all_to_all | solution.py:154
  10.7 7.2 %copy-start = (bf16[1024,256]{1,0:T(8,128)(2,1)S(1)}, bf16[1024,256]{1,0:T(8,128)(2,1)}, u32[]{:S(2)}) copy-start(bf16[1024,256]{1,0:T(8,128)(2,1)} %cotangent_ref.1) | copy-start | bytes 1572868
  10.7 7.2 %copy-start.3 = (bf16[128,256]{1,0:T(8,128)(2,1)S(1)}, bf16[128,256]{1,0:T(8,128)(2,1)}, u32[]{:S(2)}) copy-start(bf16[128,256]{1,0:T(8,128)(2,1)} %w_self_ref.1) | copy-start | bytes 196612
  10.8 7.2 %copy-start.4 = (bf16[128,256]{1,0:T(8,128)(2,1)S(1)}, bf16[128,256]{1,0:T(8,128)(2,1)}, u32[]{:S(2)}) copy-start(bf16[128,256]{1,0:T(8,128)(2,1)} %w_neigh_ref.1) | copy-start | bytes 196612

commit v2 on v1

--- a/solution.py
+++ b/solution.py
@@ -9,53 +9,85 @@
 from jax.sharding import PartitionSpec as P
 
 AXES = ("dom", "local")
+SENDS = ("local", "dom")
 LANES = 128
+CHUNKS = 4
+STEP = 256
 VMEM = pl.BlockSpec(memory_space=pltpu.VMEM)
-
-
-def call(kernel, out_shape, operands, flops, bytes_accessed, scratch=()):
+HBM = pl.BlockSpec(memory_space=pltpu.HBM)
+
+
+def call(
+    kernel,
+    out_shape,
+    operands,
+    flops,
+    bytes_accessed,
+    scratch=(),
+    places=None,
+    out=None,
+    limit=40 * 2**20,
+):
     return pl.pallas_call(
         kernel,
         out_shape=out_shape,
-        in_specs=[VMEM] * len(operands),
-        out_specs=jax.tree.map(lambda _: VMEM, out_shape),
+        in_specs=places or [VMEM] * len(operands),
+        out_specs=out or jax.tree.map(lambda _: VMEM, out_shape),
         scratch_shapes=list(scratch),
-        compiler_params=pltpu.CompilerParams(vmem_limit_bytes=40 * 2**20),
+        compiler_params=pltpu.CompilerParams(vmem_limit_bytes=limit),
         cost_estimate=pl.CostEstimate(
             flops=flops, bytes_accessed=bytes_accessed, transcendentals=0
         ),
     )(*operands)
 
 
-def serve_kernel(n_local, serve_ref, features_ref, out_ref):
+def serve_kernel(serve_hbm, features_hbm, out_ref, serve_ref, features_ref, serve_sem, sems):
     cap, n_dom = serve_ref.shape
     n_nodes = features_ref.shape[0]
+    part = n_nodes // CHUNKS
+    fetch = pltpu.make_async_copy(serve_hbm, serve_ref, serve_sem)
+    fetch.start()
+    loads = []
+    for i in range(CHUNKS):
+        rows = pl.ds(i * part, part)
+        loads.append(
+            pltpu.make_async_copy(features_hbm.at[rows, :], features_ref.at[rows, :], sems.at[i])
+        )
+        loads[-1].start()
+    fetch.wait()
     serve = serve_ref[...].astype(jnp.float32)
-    block = 128
-    for base in range(0, out_ref.shape[0], block):
-        row = base + lax.broadcasted_iota(jnp.int32, (block, n_dom), 0)
+    block = LANES
+    n_blocks = out_ref.shape[0] // block
+    indices = []
+    for b in range(n_blocks):
+        row = b * block + lax.broadcasted_iota(jnp.int32, (block, n_dom), 0)
         wanted = jnp.zeros((block, n_dom), jnp.float32)
         for c in range(cap):
             wanted = jnp.where(row % cap == c, serve[c : c + 1, :], wanted)
         group = lax.broadcasted_iota(jnp.int32, (block, n_dom), 1)
-        mine = group == row // (cap * n_local)
-        index = jnp.sum(jnp.where(mine, wanted, 0.0), axis=1, keepdims=True).astype(jnp.int32)
-        node = lax.broadcasted_iota(jnp.int32, (block, n_nodes), 1)
-        chosen = jnp.where(node == index, 1.0, 0.0).astype(jnp.bfloat16)
-        out_ref[base : base + block, :] = jnp.dot(
-            chosen, features_ref[...], preferred_element_type=jnp.float32
-        ).astype(jnp.bfloat16)
-
-
-def local_kernel(
-    n_local, cap, pick_ref, neighbours_ref, nodes_ref, features_ref, self_ref, counts_ref
-):
+        mine = group == row // cap % n_dom
+        index = jnp.sum(jnp.where(mine, wanted, 0.0), axis=1, keepdims=True)
+        indices.append(index.astype(jnp.int32))
+    sums = [jnp.zeros((block, out_ref.shape[1]), jnp.float32)] * n_blocks
+    for i in range(CHUNKS):
+        loads[i].wait()
+        node = i * part + lax.broadcasted_iota(jnp.int32, (block, part), 1)
+        for b in range(n_blocks):
+            chosen = jnp.where(node == indices[b], 1.0, 0.0).astype(jnp.bfloat16)
+            sums[b] += jnp.dot(
+                chosen, features_ref[i * part : (i + 1) * part, :], preferred_element_type=jnp.float32
+            )
+    for b in range(n_blocks):
+        out_ref[b * block : (b + 1) * block, :] = sums[b].astype(jnp.bfloat16)
+
+
+def local_kernel(pick_ref, neighbours_ref, nodes_ref, features_ref, self_ref, counts_ref):
     n_rows = counts_ref.shape[1]
     n_nodes = features_ref.shape[0]
     fanout, batch = neighbours_ref.shape
     pick = pick_ref[...]
     source = lax.broadcasted_iota(jnp.int32, pick.shape, 0)
-    place = (pick // cap) * (n_local * cap) + source * cap + pick % cap
+    place = source * (n_rows // pick.shape[0]) + pick
     nodes = nodes_ref[...].T
     for j in range(batch // LANES):
         rows = slice(j * LANES, (j + 1) * LANES)
@@ -88,27 +120,35 @@
     w_self_ref,
     w_neigh_ref,
     cotangent_ref,
-    hidden_ref,
+    hidden_hbm,
     partial_ref,
     inputs_ref,
     slope_ref,
     weights_ref,
+    hidden_ref,
+    sems,
 ):
     width = self_ref.shape[1]
     batch, units = cotangent_ref.shape
     weights_ref[:width, :] = w_self_ref[...]
     weights_ref[width:, :] = w_neigh_ref[...]
-    step = 256
-    for base in range(0, batch, step):
-        rows = slice(base, base + step)
-        inputs_ref[rows, :width] = self_ref[rows, :]
+    copies = []
+    for j in range(batch // STEP):
+        rows = slice(j * STEP, (j + 1) * STEP)
         total = jnp.dot(counts_ref[rows, :], arrived_ref[...], preferred_element_type=jnp.float32)
-        inputs_ref[rows, width:] = (total * (1.0 / fanout)).astype(jnp.bfloat16)
-        pre = jnp.dot(inputs_ref[rows, :], weights_ref[...], preferred_element_type=jnp.float32)
+        mean = (total * (1.0 / fanout)).astype(jnp.bfloat16)
+        inputs = jnp.concatenate([self_ref[rows, :], mean], axis=1)
+        inputs_ref[rows, :] = inputs
+        pre = jnp.dot(inputs, weights_ref[...], preferred_element_type=jnp.float32)
         sigma = jax.nn.sigmoid(pre)
-        hidden_ref[rows, :] = (pre * sigma).astype(jnp.bfloat16)
+        hidden = pre * sigma
+        hidden_ref[rows, :] = hidden.astype(jnp.bfloat16)
+        copies.append(
+            pltpu.make_async_copy(hidden_ref.at[rows, :], hidden_hbm.at[rows, :], sems.at[j])
+        )
+        copies[-1].start()
         slope_ref[rows, :] = (
-            cotangent_ref[rows, :].astype(jnp.float32) * sigma * (1.0 + pre * (1.0 - sigma))
+            cotangent_ref[rows, :].astype(jnp.float32) * (sigma + hidden * (1.0 - sigma))
         ).astype(jnp.bfloat16)
     terms = lax.dot_general(
         inputs_ref[...],
@@ -119,6 +159,8 @@
     terms = (terms * scale).astype(jnp.bfloat16)
     for i in range(units // LANES):
         partial_ref[i * 2 * width : (i + 1) * 2 * width, :] = terms[:, i * LANES : (i + 1) * LANES]
+    for copy in copies:
+        copy.wait()
 
 
 def unpack_kernel(packed_ref, grad_self_ref, grad_neigh_ref):
@@ -145,17 +187,25 @@
     struct = jax.ShapeDtypeStruct
 
     outgoing = call(
-        functools.partial(serve_kernel, n_local),
+        serve_kernel,
         struct((n_rows, width), bf16),
         (serve_rows.T, features),
         2 * n_rows * n_nodes * width,
         2 * n_nodes * width,
+        (
+            pltpu.VMEM(serve_rows.shape[::-1], jnp.int32),
+            pltpu.VMEM(features.shape, bf16),
+            pltpu.SemaphoreType.DMA,
+            pltpu.SemaphoreType.DMA((CHUNKS,)),
+        ),
+        [HBM, HBM],
+        limit=60 * 2**20,
     )
     arrived = lax.all_to_all(
-        outgoing.reshape(n_devices, cap, width), AXES, split_axis=0, concat_axis=0, tiled=True
+        outgoing.reshape(n_devices, cap, width), SENDS, split_axis=0, concat_axis=0, tiled=True
     ).reshape(n_rows, width)
     self_rows, counts = call(
-        functools.partial(local_kernel, n_local, cap),
+        local_kernel,
         (struct((batch, width), bf16), struct((batch, n_rows), bf16)),
         (pick_rows, neighbours.T, batch_nodes.reshape(-1, LANES), features),
         2 * batch * n_nodes * width,
@@ -172,18 +222,21 @@
             pltpu.VMEM((batch, 2 * width), bf16),
             pltpu.VMEM((batch, units), bf16),
             pltpu.VMEM((2 * width, units), bf16),
+            pltpu.VMEM((batch, units), bf16),
+            pltpu.SemaphoreType.DMA((batch // STEP,)),
         ),
+        out=(HBM, VMEM),
     )
     packed = partial.shape[0]
     share = -(-packed // n_devices)
     if share * n_devices != packed:
         partial = jnp.pad(partial, ((0, share * n_devices - packed), (0, 0)))
     pieces = lax.all_to_all(
-        partial.reshape(n_devices, share, LANES), AXES, split_axis=0, concat_axis=0, tiled=True
+        partial.reshape(n_devices, share, LANES), SENDS, split_axis=0, concat_axis=0, tiled=True
     )
     summed = jnp.sum(pieces.astype(f32), axis=0).astype(bf16)
     gathered = lax.all_to_all(
-        jnp.broadcast_to(summed, pieces.shape), AXES, split_axis=0, concat_axis=0, tiled=True
+        jnp.broadcast_to(summed, pieces.shape), SENDS, split_axis=0, concat_axis=0, tiled=True
     ).reshape(n_devices * share, LANES)
     grad_self, grad_neigh = call(
         unpack_kernel,

time: 40.5 us -> 39.4 us (0.973)
  local copies, waits for them, and re-layouts: 1.77 us -> 0.06 us
  Pallas kernels: 5.83 us -> 6.97 us
  blocking collectives: 19.8 us -> 19.3 us
    unnamed x18 -> x14, local copies, waits for them, and re-layouts: 1.75 us -> 0.04 us
    pallas_call x4, Pallas kernels: 5.83 us -> 6.97 us  [call(): pl.pallas_call(kernel, out_shape=out_shape, in_specs=places or [VMEM] * l...]
    all_to_all x2, blocking collectives: 19.8 us -> 19.3 us  [the longest x1 9.9 us: local(): lax.all_to_all(jnp.broadcast_to(summed, pieces.shape), SENDS, split_axis=...]
where the time goes in v2:
time: 39.4 us; the launch traced here: 39.1 us
  blocking collectives  19.3 us (49%)
  starting transfers between devices  7.3 us (19%)
  Pallas kernels  6.97 us (18%)
  waiting for transfers between devices  4.64 us (12%)
  between operations  0.76 us (2%)
    all_to_all x1, blocking collectives, local(): lax.all_to_all(jnp.broadcast_to(summed, pieces.shape), SENDS, split_axis=...  9.9 us
    all_to_all x1, blocking collectives, local(): lax.all_to_all(partial.reshape(n_devices, share, LANES), SENDS, split_axi...  9.44 us
    all_to_all x1, starting transfers between devices, local(): lax.all_to_all(outgoing.reshape(n_devices, cap, width), SENDS, split_axis...  7.3 us
    pallas_call x4, Pallas kernels, call(): pl.pallas_call(kernel, out_shape=out_shape, in_specs=places or [VMEM] * l...  6.97 us
    all_to_all x1, waiting for transfers between devices, local(): lax.all_to_all(outgoing.reshape(n_devices, cap, width), SENDS, split_axis...  4.64 us
  transfers between devices with their start and end apart: 1, of which 1 were waited for; matrix products, arithmetic and copies ran while one was open for 0% of the time, Pallas kernels for 6%

profile of v2, /device:TPU:0, one launch (start us, length us, event | category | flops | bytes accessed | tf_op | source)
XLA Modules:
  0.0 39.1 jit_solution(7471788735148583002)
XLA Ops:
  0.6 0.0 copy-start.1
  0.6 0.0 copy-start.6
  0.7 2.3 %shard_map.103 = bf16[128,128]{1,0:T(8,128)(2,1)} custom-call(s32[4,8]{1,0:T(4,128)} %bitcast.13, bf16[2048,128]{1,0:T(8,128)(2,1)} %features_ref.1), custom_call_target="tpu_custom_call" | custom-call | flops 67108864 | bytes 524288 | tf_op jit(solution)/shard_map/pallas_call | solution.py:31
  3.0 0.0 copy-start.4
  3.0 0.0 copy-start.5
  3.0 7.3 %all-to-all-start = ((bf16[32,4,128]{2,1,0:T(4,128)(2,1)}), bf16[32,4,128]{2,1,0:T(4,128)(2,1)S(1)}, u32[]{:S(2)}, u32[]{:S(2)}) async-start(bf16[32,4,128]{2,1,0:T(4,128)(2,1)} %bitcast.12), calls=%async_computation | async-start | bytes 65536 | tf_op jit(solution)/shard_map/all_to_all | solution.py:204
  10.3 0.0 copy-done.1
  10.3 0.0 copy-done.6
  10.3 0.0 copy-done.4
  10.3 0.0 copy-done.5
  10.3 0.0 copy-start
  10.4 0.0 copy-start.2
  10.4 0.0 copy-start.3
  10.4 2.5 %shard_map.104 = (bf16[1024,128]{1,0:T(8,128)(2,1)S(1)}, bf16[1024,128]{1,0:T(8,128)(2,1)S(1)}) custom-call(s32[4,128]{1,0:T(4,128)S(1)} %copy-done.6, s32[15,1024]{1,0:T(8,128)S(1)} %bitcast.10, s32[8,128]{1,0:T(8,128)S(1)} %bitcast.11, bf16[2048,128]{1,0:T(8,128)(2,1)S(1)} %copy-done.1), custom_call_target="tpu_custom_call" | custom-call | flops 536870912 | bytes 524288 | tf_op jit(solution)/shard_map/pallas_call | solution.py:31
  12.8 4.6 %all-to-all-done = bf16[32,4,128]{2,1,0:T(4,128)(2,1)S(1)} async-done(((bf16[32,4,128]{2,1,0:T(4,128)(2,1)}), bf16[32,4,128]{2,1,0:T(4,128)(2,1)S(1)}, u32[]{:S(2)}, u32[]{:S(2)}) %all-to-all-start) | async-done | bytes 32800 | tf_op jit(solution)/shard_map/all_to_all | solution.py:204
  17.5 0.0 copy-done
  17.5 0.0 copy-done.2
  17.5 0.0 copy-done.3
  17.5 1.5 %shard_map.105 = (bf16[1024,256]{1,0:T(8,128)(2,1)}, bf16[512,128]{1,0:T(8,128)(2,1)S(1)}) custom-call(bf16[128,128]{1,0:T(8,128)(2,1)S(1)} %bitcast.8, bf16[1024,128]{1,0:T(8,128)(2,1)S(1)} %get-tuple-element.9.counts_ref, bf16[1024,128]{1,0:T(8,128)(2,1)S(1)} %get-tuple-element.10.self_ref, bf16[128,256]{1,0:T(8,128)(2,1)S(1)} %copy-done.2, ...), custom_call_target="tpu_custom_call" | custom-call | flops 268435456 | bytes 1048576 | tf_op jit(solution)/shard_map/pallas_call | solution.py:31
  19.0 9.4 %all_to_all.15 = bf16[32,16,128]{2,1,0:T(8,128)(2,1)S(1)} all-to-all(bf16[32,16,128]{2,1,0:T(8,128)(2,1)S(1)} %bitcast.9), channel_id=1, replica_groups=mesh['dom'=8,'local'=4] {'local','dom'}, dimensions={0} | all-to-all | bytes 262144 | tf_op jit(solution)/shard_map/all_to_all | solution.py:234
  28.5 9.9 %all_to_all.16 = bf16[32,16,128]{2,1,0:T(8,128)(2,1)S(1)} all-to-all(bf16[32,16,128]{2,1,0:T(8,128)(2,1)S(1)} %broadcast_in_dim.3), channel_id=1, replica_groups=mesh['dom'=8,'local'=4] {'local','dom'}, dimensions={0} | all-to-all | bytes 262144 | tf_op jit(solution)/shard_map/all_to_all | solution.py:238
  38.4 0.7 %shard_map.106 = (f32[128,256]{1,0:T(8,128)}, f32[128,256]{1,0:T(8,128)}) custom-call(bf16[512,128]{1,0:T(8,128)(2,1)S(1)} %bitcast.7), custom_call_target="tpu_custom_call" | custom-call | bytes 393216 | tf_op jit(solution)/shard_map/pallas_call | solution.py:31
  (2 shorter events, 0.1 us)
Async XLA Ops:
  0.6 9.7 %copy-start.1 = (bf16[2048,128]{1,0:T(8,128)(2,1)S(1)}, bf16[2048,128]{1,0:T(8,128)(2,1)}, u32[]{:S(2)}) copy-start(bf16[2048,128]{1,0:T(8,128)(2,1)} %features_ref.1) | copy-start | bytes 1572868
  0.6 9.7 %copy-start.6 = (s32[4,128]{1,0:T(4,128)S(1)}, s32[4,128]{1,0:T(4,128)}, u32[]{:S(2)}) copy-start(s32[4,128]{1,0:T(4,128)} %pick_ref.1) | copy-start | bytes 6148
  3.0 7.4 %copy-start.4 = (s32[1024,15]{0,1:T(8,128)S(1)}, s32[1024,15]{0,1:T(8,128)}, u32[]{:S(2)}) copy-start(s32[1024,15]{0,1:T(8,128)} %param.11) | copy-start | bytes 184324
  3.0 7.4 %copy-start.5 = (s32[1024]{0:T(1024)S(1)}, s32[1024]{0:T(1024)}, u32[]{:S(2)}) copy-start(s32[1024]{0:T(1024)} %param.12) | copy-start | bytes 12292
  3.0 14.5 %all-to-all-start = ((bf16[32,4,128]{2,1,0:T(4,128)(2,1)}), bf16[32,4,128]{2,1,0:T(4,128)(2,1)S(1)}, u32[]{:S(2)}, u32[]{:S(2)}) async-start(bf16[32,4,128]{2,1,0:T(4,128)(2,1)} %bitcast.12), calls=%async_computation | async-start | bytes 65536 | tf_op jit(solution)/shard_map/all_to_all | solution.py:204
  10.3 7.1 %copy-start = (bf16[1024,256]{1,0:T(8,128)(2,1)S(1)}, bf16[1024,256]{1,0:T(8,128)(2,1)}, u32[]{:S(2)}) copy-start(bf16[1024,256]{1,0:T(8,128)(2,1)} %cotangent_ref.1) | copy-start | bytes 1572868
  10.4 7.1 %copy-start.2 = (bf16[128,256]{1,0:T(8,128)(2,1)S(1)}, bf16[128,256]{1,0:T(8,128)(2,1)}, u32[]{:S(2)}) copy-start(bf16[128,256]{1,0:T(8,128)(2,1)} %w_self_ref.1) | copy-start | bytes 196612
  10.4 7.1 %copy-start.3 = (bf16[128,256]{1,0:T(8,128)(2,1)S(1)}, bf16[128,256]{1,0:T(8,128)(2,1)}, u32[]{:S(2)}) copy-start(bf16[128,256]{1,0:T(8,128)(2,1)} %w_neigh_ref.1) | copy-start | bytes 196612

commit v3 on v1

v3 whole, which is shorter than its diff:
```python
import functools
import math

import jax
import jax.numpy as jnp
from jax import lax
from jax.experimental import pallas as pl
from jax.experimental.pallas import tpu as pltpu
from jax.sharding import PartitionSpec as P

AXES = ("dom", "local")
SENDS = ("local", "dom")
LANES = 128
STEP = 512
PARTS = 1
VMEM = pl.BlockSpec(memory_space=pltpu.VMEM)
HBM = pl.BlockSpec(memory_space=pltpu.HBM)


def call(
    kernel,
    out_shape,
    operands,
    flops,
    bytes_accessed,
    scratch=(),
    places=None,
    out=None,
):
    return pl.pallas_call(
        kernel,
        out_shape=out_shape,
        in_specs=places or [VMEM] * len(operands),
        out_specs=out or jax.tree.map(lambda _: VMEM, out_shape),
        scratch_shapes=list(scratch),
        compiler_params=pltpu.CompilerParams(vmem_limit_bytes=40 * 2**20),
        cost_estimate=pl.CostEstimate(
            flops=flops, bytes_accessed=bytes_accessed, transcendentals=0
        ),
    )(*operands)


def serve_kernel(
    serve_hbm,
    features_hbm,
    pick_hbm,
    neighbours_hbm,
    nodes_hbm,
    out_ref,
    features_ref,
    pick_ref,
    neighbours_ref,
    nodes_ref,
    serve_ref,
    sems,
):
    cap, n_dom = serve_ref.shape
    n_nodes = features_ref.shape[0]
    pairs = (
        (serve_hbm, serve_ref),
        (features_hbm, features_ref),
        (pick_hbm, pick_ref),
        (neighbours_hbm, neighbours_ref),
        (nodes_hbm, nodes_ref),
    )
    fetches = [pltpu.make_async_copy(*pair, sems.at[i]) for i, pair in enumerate(pairs)]
    for fetch in fetches:
        fetch.start()
    fetches[0].wait()
    serve = serve_ref[...].astype(jnp.float32)
    block = LANES
    picked = []
    for base in range(0, out_ref.shape[0], block):
        row = base + lax.broadcasted_iota(jnp.int32, (block, n_dom), 0)
        wanted = jnp.zeros((block, n_dom), jnp.float32)
        for c in range(cap):
            wanted = jnp.where(row % cap == c, serve[c : c + 1, :], wanted)
        group = lax.broadcasted_iota(jnp.int32, (block, n_dom), 1)
        mine = group == row // cap % n_dom
        index = jnp.sum(jnp.where(mine, wanted, 0.0), axis=1, keepdims=True).astype(jnp.int32)
        node = lax.broadcasted_iota(jnp.int32, (block, n_nodes), 1)
        picked.append(jnp.where(node == index, 1.0, 0.0).astype(jnp.bfloat16))
    for fetch in fetches[1:]:
        fetch.wait()
    for i, chosen in enumerate(picked):
        out_ref[i * block : (i + 1) * block, :] = jnp.dot(
            chosen, features_ref[...], preferred_element_type=jnp.float32
        ).astype(jnp.bfloat16)


def local_kernel(pick_ref, neighbours_ref, nodes_ref, features_ref, self_ref, counts_ref):
    n_rows = counts_ref.shape[1]
    n_nodes, width = features_ref.shape
    fanout, batch = neighbours_ref.shape
    bf16, i16 = jnp.bfloat16, jnp.int16
    one, zero = bf16(1), bf16(0)
    pick = pick_ref[...]
    source = lax.broadcasted_iota(jnp.int32, pick.shape, 0)
    place = source * (n_rows // pick.shape[0]) + pick
    nodes = nodes_ref[...].T
    half = n_nodes // 2
    halves = jnp.concatenate([features_ref[:half, :], features_ref[half:, :]], axis=1)
    node = lax.broadcasted_iota(jnp.int32, (LANES, half), 1)
    for j in range(batch // LANES):
        rows = slice(j * LANES, (j + 1) * LANES)
        near = neighbours_ref[:, rows]
        lane, tile = near % LANES, near // LANES
        where = jnp.zeros_like(near)
        for m in range(pick.shape[0]):
            table = jnp.broadcast_to(place[m : m + 1, :], near.shape)
            found = jnp.take_along_axis(table, lane, axis=1)
            where = jnp.where(tile == m, found, where)
        where = where.astype(i16)
        for base in range(0, n_rows, LANES):
            row = (base + lax.broadcasted_iota(jnp.int32, (LANES, LANES), 0)).astype(i16)
            count = jnp.zeros((LANES, LANES), bf16)
            for k in range(fanout):
                hit = jnp.broadcast_to(where[k : k + 1, :], (LANES, LANES)) == row
                count += jnp.where(hit, one, zero)
            counts_ref[rows, base : base + LANES] = count.T
        mine = nodes[:, j : j + 1]
        upper = mine >= half
        chosen = jnp.where(node == jnp.where(upper, mine - half, mine), 1.0, 0.0).astype(bf16)
        both = jnp.dot(chosen, halves, preferred_element_type=jnp.float32)
        self_ref[rows, :] = jnp.where(upper, both[:, width:], both[:, :width]).astype(bf16)


def layer_kernel(
    fanout,
    scale,
    arrived_ref,
    counts_ref,
    self_ref,
    w_self_ref,
    w_neigh_ref,
    cotangent_ref,
    hidden_ref,
    partial_ref,
    inputs_ref,
    slope_ref,
):
    width = self_ref.shape[1]
    batch, units = cotangent_ref.shape
    weights = jnp.concatenate([w_self_ref[...], w_neigh_ref[...]], axis=0)
    for base in range(0, batch, STEP):
        rows = slice(base, base + STEP)
        total = jnp.dot(counts_ref[rows, :], arrived_ref[...], preferred_element_type=jnp.float32)
        mean = (total * (1.0 / fanout)).astype(jnp.bfloat16)
        inputs = jnp.concatenate([self_ref[rows, :], mean], axis=1)
        inputs_ref[rows, :] = inputs
        pre = jnp.dot(inputs, weights, preferred_element_type=jnp.float32)
        sigma = jax.nn.sigmoid(pre)
        hidden = pre * sigma
        hidden_ref[rows, :] = hidden.astype(jnp.bfloat16)
        slope_ref[rows, :] = (
            cotangent_ref[rows, :].astype(jnp.float32) * (sigma + hidden * (1.0 - sigma))
        ).astype(jnp.bfloat16)
    terms = lax.dot_general(
        inputs_ref[...],
        slope_ref[...],
        (((0,), (0,)), ((), ())),
        preferred_element_type=jnp.float32,
    )
    terms = (terms * scale).astype(jnp.bfloat16)
    for i in range(units // LANES):
        partial_ref[i * 2 * width : (i + 1) * 2 * width, :] = terms[:, i * LANES : (i + 1) * LANES]


def finish_kernel(
    packed_ref, hidden_ref, hidden_hbm, grad_self_hbm, grad_neigh_hbm, grad_self_ref, grad_neigh_ref, sems
):
    width, units = grad_self_ref.shape
    part = hidden_ref.shape[0] // PARTS
    copies = []
    for i in range(PARTS):
        rows = pl.ds(i * part, part)
        copies.append(
            pltpu.make_async_copy(hidden_ref.at[rows, :], hidden_hbm.at[rows, :], sems.at[i])
        )
        copies[-1].start()
    for j, (ref, hbm) in enumerate(((grad_self_ref, grad_self_hbm), (grad_neigh_ref, grad_neigh_hbm))):
        for i in range(units // LANES):
            base = (2 * i + j) * width
            ref[:, i * LANES : (i + 1) * LANES] = packed_ref[base : base + width, :].astype(
                jnp.float32
            )
        copies.append(pltpu.make_async_copy(ref, hbm, sems.at[PARTS + j]))
        copies[-1].start()
    for copy in copies:
        copy.wait()


def local(features, serve_rows, pick_rows, neighbours, batch_nodes, w_self, w_neigh, cotangent):
    n_dom = lax.axis_size("dom")
    n_local = lax.axis_size("local")
    n_devices = n_dom * n_local
    n_nodes, width = features.shape
    batch, fanout = neighbours.shape
    units = w_self.shape[1]
    cap = serve_rows.shape[1]
    n_rows = n_devices * cap
    bf16, f32 = jnp.bfloat16, jnp.float32
    struct = jax.ShapeDtypeStruct

    own = (serve_rows.T, features, pick_rows, neighbours.T, batch_nodes.reshape(-1, LANES))
    held = [pltpu.VMEM(x.shape, x.dtype) for x in own]
    outgoing, *held = call(
        serve_kernel,
        (pltpu.VMEM((n_rows, width), bf16), held[1], held[2], held[3], held[4]),
        [pltpu.with_memory_space_constraint(x, pltpu.HBM) for x in own],
        2 * n_rows * n_nodes * width,
        2 * n_nodes * width,
        (held[0], pltpu.SemaphoreType.DMA((len(own),))),
        [HBM] * len(own),
    )
    arrived = lax.all_to_all(
        outgoing.reshape(n_devices, cap, width), SENDS, split_axis=0, concat_axis=0, tiled=True
    ).reshape(n_rows, width)
    self_rows, counts = call(
        local_kernel,
        (struct((batch, width), bf16), struct((batch, n_rows), bf16)),
        (held[1], held[2], held[3], held[0]),
        2 * batch * n_nodes * width,
        2 * n_nodes * width,
    )
    scale = 1.0 / math.sqrt(n_devices * batch)
    hidden, partial = call(
        functools.partial(layer_kernel, fanout, scale),
        (
            pltpu.VMEM((batch, units), bf16),
            pltpu.VMEM((2 * width * units // LANES, LANES), bf16),
        ),
        (arrived, counts, self_rows, w_self, w_neigh, cotangent),
        8 * batch * width * units,
        4 * batch * units,
        (pltpu.VMEM((batch, 2 * width), bf16), pltpu.VMEM((batch, units), bf16)),
    )
    packed = partial.shape[0]
    share = -(-packed // n_devices)
    if share * n_devices != packed:
        partial = jnp.pad(partial, ((0, share * n_devices - packed), (0, 0)))
    pieces = lax.all_to_all(
        partial.reshape(n_devices, share, LANES), SENDS, split_axis=0, concat_axis=0, tiled=True
    )
    summed = jnp.sum(pieces.astype(f32), axis=0).astype(bf16)
    gathered = lax.all_to_all(
        jnp.broadcast_to(summed, pieces.shape), SENDS, split_axis=0, concat_axis=0, tiled=True
    ).reshape(n_devices * share, LANES)
    grad = struct((width, units), f32)
    return call(
        finish_kernel,
        (struct(hidden.shape, bf16), grad, grad),
        (gathered, hidden),
        0,
        4 * batch * units + 12 * width * units,
        (
            pltpu.VMEM(grad.shape, f32),
            pltpu.VMEM(grad.shape, f32),
            pltpu.SemaphoreType.DMA((PARTS + 2,)),
        ),
        out=(HBM, HBM, HBM),
    )


def solution(mesh):
    rows = P(AXES, None)
    return jax.shard_map(
        local,
        mesh=mesh,
        in_specs=(rows, rows, rows, rows, P(AXES), P(), P(), rows),
        out_specs=(rows, P(), P()),
        check_vma=False,
    )
```

time: 40.5 us -> 38.5 us (0.951)
  local copies, waits for them, and re-layouts: 1.77 us -> 0.04 us
  waiting for transfers between devices: 4.71 us -> 5.65 us
  Pallas kernels: 5.83 us -> 5.25 us
  blocking collectives: 19.8 us -> 19.3 us
    unnamed x18 -> x6, local copies, waits for them, and re-layouts: 1.75 us -> 0.02 us
    all_to_all x1, waiting for transfers between devices: 4.71 us -> 5.65 us  [local(): lax.all_to_all(outgoing.reshape(n_devices, cap, width), SENDS, split_axis...]
    pallas_call x4, Pallas kernels: 5.83 us -> 5.25 us  [call(): pl.pallas_call(kernel, out_shape=out_shape, in_specs=places or [VMEM] * l...]
    all_to_all x2, blocking collectives: 19.8 us -> 19.3 us  [the longest x1 9.9 us: local(): lax.all_to_all(jnp.broadcast_to(summed, pieces.shape), SENDS, split_axis=...]
  transfers between devices with their start and end apart: 1 -> 1, of which waited for: 1 -> 1; matrix products, arithmetic and copies ran while one was open for 0% -> 0% of each run, Pallas kernels for 6% -> 4%
where the time goes in v3:
time: 38.5 us; the launch traced here: 38.3 us
  blocking collectives  19.3 us (50%)
  starting transfers between devices  7.3 us (19%)
  waiting for transfers between devices  5.65 us (15%)
  Pallas kernels  5.25 us (14%)
  between operations  0.7 us (2%)
    all_to_all x1, blocking collectives, local(): lax.all_to_all(jnp.broadcast_to(summed, pieces.shape), SENDS, split_axis=...  9.9 us
    all_to_all x1, blocking collectives, local(): lax.all_to_all(partial.reshape(n_devices, share, LANES), SENDS, split_axi...  9.44 us
    all_to_all x1, starting transfers between devices, local(): lax.all_to_all(outgoing.reshape(n_devices, cap, width), SENDS, split_axis...  7.3 us
    all_to_all x1, waiting for transfers between devices, local(): lax.all_to_all(outgoing.reshape(n_devices, cap, width), SENDS, split_axis...  5.65 us
    pallas_call x4, Pallas kernels, call(): pl.pallas_call(kernel, out_shape=out_shape, in_specs=places or [VMEM] * l...  5.25 us
  transfers between devices with their start and end apart: 1, of which 1 were waited for; matrix products, arithmetic and copies ran while one was open for 0% of the time, Pallas kernels for 4%

profile of v3, /device:TPU:0, one launch (start us, length us, event | category | flops | bytes accessed | tf_op | source)
XLA Modules:
  0.0 38.3 jit_solution(9210802007928452145)
XLA Ops:
  0.6 2.0 %shard_map.103 = (bf16[128,128]{1,0:T(8,128)(2,1)}, bf16[2048,128]{1,0:T(8,128)(2,1)S(1)}, s32[4,128]{1,0:T(4,128)S(1)}, s32[15,1024]{1,0:T(8,128)S(1)}, s32[8,128]{1,0:T(8,128)S(1)}) custom-call(s32[4,8]{1,0:T(4,128)} %bitcast.12, bf16[2048,128]{1,0:T(8,128)(2,1)} %features_hbm.1, s32[4,128]{1,0:T(4,128)} %pick_hbm.1, s32[15,1024]{1,0:T(8,128)} %bitcast.10, ...), custom_call_target="tpu_custom_call" | custom-call | flops 67108864 | bytes 524288 | tf_op jit(solution)/shard_map/pallas_call | solution.py:30
  2.6 7.3 %all-to-all-start = ((bf16[32,4,128]{2,1,0:T(4,128)(2,1)}), bf16[32,4,128]{2,1,0:T(4,128)(2,1)S(1)}, u32[]{:S(2)}, u32[]{:S(2)}) async-start(bf16[32,4,128]{2,1,0:T(4,128)(2,1)} %bitcast.3), calls=%async_computation | async-start | bytes 65536 | tf_op jit(solution)/shard_map/all_to_all | solution.py:216
  10.0 0.0 copy-start
  10.0 0.0 copy-start.1
  10.0 0.0 copy-start.2
  10.0 1.5 %shard_map.104 = (bf16[1024,128]{1,0:T(8,128)(2,1)S(1)}, bf16[1024,128]{1,0:T(8,128)(2,1)S(1)}) custom-call(s32[4,128]{1,0:T(4,128)S(1)} %get-tuple-element.13.pick_ref, s32[15,1024]{1,0:T(8,128)S(1)} %get-tuple-element.14.neighbours_ref, s32[8,128]{1,0:T(8,128)S(1)} %get-tuple-element.15.nodes_ref, bf16[2048,128]{1,0:T(8,128)(2,1)S(1)} %get-tuple-element.16.features_ref), custom_call_target="tpu_custom_call" | custom-call | flops 536870912 | bytes 524288 | tf_op jit(solution)/shard_map/pallas_call | solution.py:30
  11.5 5.6 %all-to-all-done = bf16[32,4,128]{2,1,0:T(4,128)(2,1)S(1)} async-done(((bf16[32,4,128]{2,1,0:T(4,128)(2,1)}), bf16[32,4,128]{2,1,0:T(4,128)(2,1)S(1)}, u32[]{:S(2)}, u32[]{:S(2)}) %all-to-all-start) | async-done | bytes 32800 | tf_op jit(solution)/shard_map/all_to_all | solution.py:216
  17.1 0.0 copy-done
  17.1 0.0 copy-done.1
  17.1 0.0 copy-done.2
  17.2 0.9 %shard_map.105 = (bf16[1024,256]{1,0:T(8,128)(2,1)S(1)}, bf16[512,128]{1,0:T(8,128)(2,1)S(1)}) custom-call(bf16[128,128]{1,0:T(8,128)(2,1)S(1)} %bitcast.8, bf16[1024,128]{1,0:T(8,128)(2,1)S(1)} %get-tuple-element.17.counts_ref, bf16[1024,128]{1,0:T(8,128)(2,1)S(1)} %get-tuple-element.18.self_ref, bf16[128,256]{1,0:T(8,128)(2,1)S(1)} %copy-done.1, ...), custom_call_target="tpu_custom_call" | custom-call | flops 268435456 | bytes 1048576 | tf_op jit(solution)/shard_map/pallas_call | solution.py:30
  18.0 9.4 %all_to_all.15 = bf16[32,16,128]{2,1,0:T(8,128)(2,1)S(1)} all-to-all(bf16[32,16,128]{2,1,0:T(8,128)(2,1)S(1)} %bitcast.9), channel_id=1, replica_groups=mesh['dom'=8,'local'=4] {'local','dom'}, dimensions={0} | all-to-all | bytes 262144 | tf_op jit(solution)/shard_map/all_to_all | solution.py:242
  27.5 9.9 %all_to_all.16 = bf16[32,16,128]{2,1,0:T(8,128)(2,1)S(1)} all-to-all(bf16[32,16,128]{2,1,0:T(8,128)(2,1)S(1)} %broadcast_in_dim.3), channel_id=1, replica_groups=mesh['dom'=8,'local'=4] {'local','dom'}, dimensions={0} | all-to-all | bytes 262144 | tf_op jit(solution)/shard_map/all_to_all | solution.py:246
  37.4 0.9 %shard_map.106 = (bf16[1024,256]{1,0:T(8,128)(2,1)}, f32[128,256]{1,0:T(8,128)}, f32[128,256]{1,0:T(8,128)}) custom-call(bf16[512,128]{1,0:T(8,128)(2,1)S(1)} %bitcast.7, bf16[1024,256]{1,0:T(8,128)(2,1)S(1)} %get-tuple-element.20.hidden_ref), custom_call_target="tpu_custom_call" | custom-call | bytes 1441792 | tf_op jit(solution)/shard_map/pallas_call | solution.py:30
  (2 shorter events, 0.1 us)
Async XLA Ops:
  2.6 14.5 %all-to-all-start = ((bf16[32,4,128]{2,1,0:T(4,128)(2,1)}), bf16[32,4,128]{2,1,0:T(4,128)(2,1)S(1)}, u32[]{:S(2)}, u32[]{:S(2)}) async-start(bf16[32,4,128]{2,1,0:T(4,128)(2,1)} %bitcast.3), calls=%async_computation | async-start | bytes 65536 | tf_op jit(solution)/shard_map/all_to_all | solution.py:216
  10.0 7.2 %copy-start = (bf16[1024,256]{1,0:T(8,128)(2,1)S(1)}, bf16[1024,256]{1,0:T(8,128)(2,1)}, u32[]{:S(2)}) copy-start(bf16[1024,256]{1,0:T(8,128)(2,1)} %cotangent_ref.1) | copy-start | bytes 1572868
  10.0 7.2 %copy-start.1 = (bf16[128,256]{1,0:T(8,128)(2,1)S(1)}, bf16[128,256]{1,0:T(8,128)(2,1)}, u32[]{:S(2)}) copy-start(bf16[128,256]{1,0:T(8,128)(2,1)} %w_self_ref.1) | copy-start | bytes 196612
  10.0 7.2 %copy-start.2 = (bf16[128,256]{1,0:T(8,128)(2,1)S(1)}, bf16[128,256]{1,0:T(8,128)(2,1)}, u32[]{:S(2)}) copy-start(bf16[128,256]{1,0:T(8,128)(2,1)} %w_neigh_ref.1) | copy-start | bytes 196612

commit v4 on v3

--- a/solution.py
+++ b/solution.py
@@ -11,8 +11,6 @@
 AXES = ("dom", "local")
 SENDS = ("local", "dom")
 LANES = 128
-STEP = 512
-PARTS = 1
 VMEM = pl.BlockSpec(memory_space=pltpu.VMEM)
 HBM = pl.BlockSpec(memory_space=pltpu.HBM)
 
@@ -140,21 +138,19 @@
     slope_ref,
 ):
     width = self_ref.shape[1]
-    batch, units = cotangent_ref.shape
+    units = cotangent_ref.shape[1]
     weights = jnp.concatenate([w_self_ref[...], w_neigh_ref[...]], axis=0)
-    for base in range(0, batch, STEP):
-        rows = slice(base, base + STEP)
-        total = jnp.dot(counts_ref[rows, :], arrived_ref[...], preferred_element_type=jnp.float32)
-        mean = (total * (1.0 / fanout)).astype(jnp.bfloat16)
-        inputs = jnp.concatenate([self_ref[rows, :], mean], axis=1)
-        inputs_ref[rows, :] = inputs
-        pre = jnp.dot(inputs, weights, preferred_element_type=jnp.float32)
-        sigma = jax.nn.sigmoid(pre)
-        hidden = pre * sigma
-        hidden_ref[rows, :] = hidden.astype(jnp.bfloat16)
-        slope_ref[rows, :] = (
-            cotangent_ref[rows, :].astype(jnp.float32) * (sigma + hidden * (1.0 - sigma))
-        ).astype(jnp.bfloat16)
+    total = jnp.dot(counts_ref[...], arrived_ref[...], preferred_element_type=jnp.float32)
+    mean = (total * (1.0 / fanout)).astype(jnp.bfloat16)
+    inputs = jnp.concatenate([self_ref[...], mean], axis=1)
+    inputs_ref[...] = inputs
+    pre = jnp.dot(inputs, weights, preferred_element_type=jnp.float32)
+    sigma = jax.nn.sigmoid(pre)
+    hidden = pre * sigma
+    hidden_ref[...] = hidden.astype(jnp.bfloat16)
+    slope_ref[...] = (
+        cotangent_ref[...].astype(jnp.float32) * (sigma + hidden * (1.0 - sigma))
+    ).astype(jnp.bfloat16)
     terms = lax.dot_general(
         inputs_ref[...],
         slope_ref[...],
@@ -170,21 +166,15 @@
     packed_ref, hidden_ref, hidden_hbm, grad_self_hbm, grad_neigh_hbm, grad_self_ref, grad_neigh_ref, sems
 ):
     width, units = grad_self_ref.shape
-    part = hidden_ref.shape[0] // PARTS
-    copies = []
-    for i in range(PARTS):
-        rows = pl.ds(i * part, part)
-        copies.append(
-            pltpu.make_async_copy(hidden_ref.at[rows, :], hidden_hbm.at[rows, :], sems.at[i])
-        )
-        copies[-1].start()
+    copies = [pltpu.make_async_copy(hidden_ref, hidden_hbm, sems.at[0])]
+    copies[0].start()
     for j, (ref, hbm) in enumerate(((grad_self_ref, grad_self_hbm), (grad_neigh_ref, grad_neigh_hbm))):
         for i in range(units // LANES):
             base = (2 * i + j) * width
             ref[:, i * LANES : (i + 1) * LANES] = packed_ref[base : base + width, :].astype(
                 jnp.float32
             )
-        copies.append(pltpu.make_async_copy(ref, hbm, sems.at[PARTS + j]))
+        copies.append(pltpu.make_async_copy(ref, hbm, sems.at[1 + j]))
         copies[-1].start()
     for copy in copies:
         copy.wait()
@@ -256,7 +246,7 @@
         (
             pltpu.VMEM(grad.shape, f32),
             pltpu.VMEM(grad.shape, f32),
-            pltpu.SemaphoreType.DMA((PARTS + 2,)),
+            pltpu.SemaphoreType.DMA((3,)),
         ),
         out=(HBM, HBM, HBM),
     )

time: 38.5 us -> 38.5 us (level)
  no operation moved by 1% of the time
where the time goes in v4:
time: 38.5 us; the launch traced here: 38.3 us
  blocking collectives  19.3 us (50%)
  starting transfers between devices  7.3 us (19%)
  waiting for transfers between devices  5.65 us (15%)
  Pallas kernels  5.19 us (13%)
  between operations  0.7 us (2%)
    all_to_all x1, blocking collectives, local(): lax.all_to_all(jnp.broadcast_to(summed, pieces.shape), SENDS, split_axis=...  9.9 us
    all_to_all x1, blocking collectives, local(): lax.all_to_all(partial.reshape(n_devices, share, LANES), SENDS, split_axi...  9.44 us
    all_to_all x1, starting transfers between devices, local(): lax.all_to_all(outgoing.reshape(n_devices, cap, width), SENDS, split_axis...  7.3 us
    all_to_all x1, waiting for transfers between devices, local(): lax.all_to_all(outgoing.reshape(n_devices, cap, width), SENDS, split_axis...  5.65 us
    pallas_call x4, Pallas kernels, call(): pl.pallas_call(kernel, out_shape=out_shape, in_specs=places or [VMEM] * l...  5.19 us
  transfers between devices with their start and end apart: 1, of which 1 were waited for; matrix products, arithmetic and copies ran while one was open for 0% of the time, Pallas kernels for 4%

profile of v4, /device:TPU:0, one launch (start us, length us, event | category | flops | bytes accessed | tf_op | source)
XLA Modules:
  0.0 38.3 jit_solution(3661768221559894025)
XLA Ops:
  0.6 2.0 %shard_map.103 = (bf16[128,128]{1,0:T(8,128)(2,1)}, bf16[2048,128]{1,0:T(8,128)(2,1)S(1)}, s32[4,128]{1,0:T(4,128)S(1)}, s32[15,1024]{1,0:T(8,128)S(1)}, s32[8,128]{1,0:T(8,128)S(1)}) custom-call(s32[4,8]{1,0:T(4,128)} %bitcast.12, bf16[2048,128]{1,0:T(8,128)(2,1)} %features_hbm.1, s32[4,128]{1,0:T(4,128)} %pick_hbm.1, s32[15,1024]{1,0:T(8,128)} %bitcast.10, ...), custom_call_target="tpu_custom_call" | custom-call | flops 67108864 | bytes 524288 | tf_op jit(solution)/shard_map/pallas_call | solution.py:28
  2.6 7.3 %all-to-all-start = ((bf16[32,4,128]{2,1,0:T(4,128)(2,1)}), bf16[32,4,128]{2,1,0:T(4,128)(2,1)S(1)}, u32[]{:S(2)}, u32[]{:S(2)}) async-start(bf16[32,4,128]{2,1,0:T(4,128)(2,1)} %bitcast.3), calls=%async_computation | async-start | bytes 65536 | tf_op jit(solution)/shard_map/all_to_all | solution.py:206
  10.0 0.0 copy-start
  10.0 0.0 copy-start.1
  10.0 0.0 copy-start.2
  10.0 1.5 %shard_map.104 = (bf16[1024,128]{1,0:T(8,128)(2,1)S(1)}, bf16[1024,128]{1,0:T(8,128)(2,1)S(1)}) custom-call(s32[4,128]{1,0:T(4,128)S(1)} %get-tuple-element.13.pick_ref, s32[15,1024]{1,0:T(8,128)S(1)} %get-tuple-element.14.neighbours_ref, s32[8,128]{1,0:T(8,128)S(1)} %get-tuple-element.15.nodes_ref, bf16[2048,128]{1,0:T(8,128)(2,1)S(1)} %get-tuple-element.16.features_ref), custom_call_target="tpu_custom_call" | custom-call | flops 536870912 | bytes 524288 | tf_op jit(solution)/shard_map/pallas_call | solution.py:28
  11.5 5.6 %all-to-all-done = bf16[32,4,128]{2,1,0:T(4,128)(2,1)S(1)} async-done(((bf16[32,4,128]{2,1,0:T(4,128)(2,1)}), bf16[32,4,128]{2,1,0:T(4,128)(2,1)S(1)}, u32[]{:S(2)}, u32[]{:S(2)}) %all-to-all-start) | async-done | bytes 32800 | tf_op jit(solution)/shard_map/all_to_all | solution.py:206
  17.1 0.0 copy-done
  17.1 0.0 copy-done.1
  17.1 0.0 copy-done.2
  17.2 0.8 %shard_map.105 = (bf16[1024,256]{1,0:T(8,128)(2,1)S(1)}, bf16[512,128]{1,0:T(8,128)(2,1)S(1)}) custom-call(bf16[128,128]{1,0:T(8,128)(2,1)S(1)} %bitcast.8, bf16[1024,128]{1,0:T(8,128)(2,1)S(1)} %get-tuple-element.17.counts_ref, bf16[1024,128]{1,0:T(8,128)(2,1)S(1)} %get-tuple-element.18.self_ref, bf16[128,256]{1,0:T(8,128)(2,1)S(1)} %copy-done.1, ...), custom_call_target="tpu_custom_call" | custom-call | flops 268435456 | bytes 1048576 | tf_op jit(solution)/shard_map/pallas_call | solution.py:28
  17.9 9.4 %all_to_all.15 = bf16[32,16,128]{2,1,0:T(8,128)(2,1)S(1)} all-to-all(bf16[32,16,128]{2,1,0:T(8,128)(2,1)S(1)} %bitcast.9), channel_id=1, replica_groups=mesh['dom'=8,'local'=4] {'local','dom'}, dimensions={0} | all-to-all | bytes 262144 | tf_op jit(solution)/shard_map/all_to_all | solution.py:232
  27.5 9.9 %all_to_all.16 = bf16[32,16,128]{2,1,0:T(8,128)(2,1)S(1)} all-to-all(bf16[32,16,128]{2,1,0:T(8,128)(2,1)S(1)} %broadcast_in_dim.3), channel_id=1, replica_groups=mesh['dom'=8,'local'=4] {'local','dom'}, dimensions={0} | all-to-all | bytes 262144 | tf_op jit(solution)/shard_map/all_to_all | solution.py:236
  37.4 0.9 %shard_map.106 = (bf16[1024,256]{1,0:T(8,128)(2,1)}, f32[128,256]{1,0:T(8,128)}, f32[128,256]{1,0:T(8,128)}) custom-call(bf16[512,128]{1,0:T(8,128)(2,1)S(1)} %bitcast.7, bf16[1024,256]{1,0:T(8,128)(2,1)S(1)} %get-tuple-element.20.hidden_ref), custom_call_target="tpu_custom_call" | custom-call | bytes 1441792 | tf_op jit(solution)/shard_map/pallas_call | solution.py:28
  (2 shorter events, 0.1 us)
Async XLA Ops:
  2.6 14.5 %all-to-all-start = ((bf16[32,4,128]{2,1,0:T(4,128)(2,1)}), bf16[32,4,128]{2,1,0:T(4,128)(2,1)S(1)}, u32[]{:S(2)}, u32[]{:S(2)}) async-start(bf16[32,4,128]{2,1,0:T(4,128)(2,1)} %bitcast.3), calls=%async_computation | async-start | bytes 65536 | tf_op jit(solution)/shard_map/all_to_all | solution.py:206
  10.0 7.2 %copy-start = (bf16[1024,256]{1,0:T(8,128)(2,1)S(1)}, bf16[1024,256]{1,0:T(8,128)(2,1)}, u32[]{:S(2)}) copy-start(bf16[1024,256]{1,0:T(8,128)(2,1)} %cotangent_ref.1) | copy-start | bytes 1572868
  10.0 7.2 %copy-start.1 = (bf16[128,256]{1,0:T(8,128)(2,1)S(1)}, bf16[128,256]{1,0:T(8,128)(2,1)}, u32[]{:S(2)}) copy-start(bf16[128,256]{1,0:T(8,128)(2,1)} %w_self_ref.1) | copy-start | bytes 196612
  10.0 7.2 %copy-start.2 = (bf16[128,256]{1,0:T(8,128)(2,1)S(1)}, bf16[128,256]{1,0:T(8,128)(2,1)}, u32[]{:S(2)}) copy-start(bf16[128,256]{1,0:T(8,128)(2,1)} %w_neigh_ref.1) | copy-start | bytes 196612

commit v5 on v4

--- a/solution.py
+++ b/solution.py
@@ -24,6 +24,7 @@
     scratch=(),
     places=None,
     out=None,
+    aliases={},
 ):
     return pl.pallas_call(
         kernel,
@@ -31,11 +32,60 @@
         in_specs=places or [VMEM] * len(operands),
         out_specs=out or jax.tree.map(lambda _: VMEM, out_shape),
         scratch_shapes=list(scratch),
+        input_output_aliases=aliases,
         compiler_params=pltpu.CompilerParams(vmem_limit_bytes=40 * 2**20),
         cost_estimate=pl.CostEstimate(
             flops=flops, bytes_accessed=bytes_accessed, transcendentals=0
         ),
     )(*operands)
+
+
+def waits_first():
+    return lax.axis_index("dom") < lax.axis_size("dom") * 6 // 8
+
+
+def local_work(pick_ref, neighbours_ref, nodes_ref, features_ref, self_ref, counts_ref):
+    n_rows = counts_ref.shape[1]
+    n_nodes, width = features_ref.shape
+    fanout, batch = neighbours_ref.shape
+    bf16, i16 = jnp.bfloat16, jnp.int16
+    one, zero = bf16(1), bf16(0)
+    pick = pick_ref[...]
+    source = lax.broadcasted_iota(jnp.int32, pick.shape, 0)
+    place = source * (n_rows // pick.shape[0]) + pick
+    nodes = nodes_ref[...].T
+    half = n_nodes // 2
+    halves = jnp.concatenate([features_ref[:half, :], features_ref[half:, :]], axis=1)
+    node = lax.broadcasted_iota(jnp.int32, (LANES, half), 1).astype(i16)
+    for j in range(batch // LANES):
+        mine = nodes[:, j : j + 1]
+        upper = mine >= half
+        low = jnp.broadcast_to(jnp.where(upper, mine - half, mine), (LANES, LANES)).astype(i16)
+        hit = node == jnp.concatenate([low] * (half // LANES), axis=1)
+        both = jnp.dot(jnp.where(hit, one, zero), halves, preferred_element_type=jnp.float32)
+        self_ref[j * LANES : (j + 1) * LANES, :] = jnp.where(
+            upper, both[:, width:], both[:, :width]
+        ).astype(bf16)
+    for j in range(batch // LANES):
+        rows = slice(j * LANES, (j + 1) * LANES)
+        near = neighbours_ref[:, rows]
+        lane, tile = near & (LANES - 1), near // LANES
+        where = jnp.zeros_like(near)
+        for m in range(pick.shape[0]):
+            table = jnp.broadcast_to(place[m : m + 1, :], near.shape)
+            found = jnp.take_along_axis(table, lane, axis=1)
+            where = jnp.where(tile == m, found, where)
+        where = where.astype(i16)
+        for base in range(0, n_rows, LANES):
+            row = (base + lax.broadcasted_iota(jnp.int32, (LANES, LANES), 0)).astype(i16)
+            hits = [
+                jnp.where(jnp.broadcast_to(where[k : k + 1, :], row.shape) == row, one, zero)
+                for k in range(fanout)
+            ]
+            while len(hits) > 1:
+                odd = hits[len(hits) // 2 * 2 :]
+                hits = [x + y for x, y in zip(hits[::2], hits[1::2])] + odd
+            counts_ref[rows, base : base + LANES] = hits[0].T
 
 
 def serve_kernel(
@@ -45,6 +95,8 @@
     neighbours_hbm,
     nodes_hbm,
     out_ref,
+    self_ref,
+    counts_ref,
     features_ref,
     pick_ref,
     neighbours_ref,
@@ -85,81 +137,67 @@
             chosen, features_ref[...], preferred_element_type=jnp.float32
         ).astype(jnp.bfloat16)
 
-
-def local_kernel(pick_ref, neighbours_ref, nodes_ref, features_ref, self_ref, counts_ref):
-    n_rows = counts_ref.shape[1]
-    n_nodes, width = features_ref.shape
-    fanout, batch = neighbours_ref.shape
-    bf16, i16 = jnp.bfloat16, jnp.int16
-    one, zero = bf16(1), bf16(0)
-    pick = pick_ref[...]
-    source = lax.broadcasted_iota(jnp.int32, pick.shape, 0)
-    place = source * (n_rows // pick.shape[0]) + pick
-    nodes = nodes_ref[...].T
-    half = n_nodes // 2
-    halves = jnp.concatenate([features_ref[:half, :], features_ref[half:, :]], axis=1)
-    node = lax.broadcasted_iota(jnp.int32, (LANES, half), 1)
-    for j in range(batch // LANES):
-        rows = slice(j * LANES, (j + 1) * LANES)
-        near = neighbours_ref[:, rows]
-        lane, tile = near % LANES, near // LANES
-        where = jnp.zeros_like(near)
-        for m in range(pick.shape[0]):
-            table = jnp.broadcast_to(place[m : m + 1, :], near.shape)
-            found = jnp.take_along_axis(table, lane, axis=1)
-            where = jnp.where(tile == m, found, where)
-        where = where.astype(i16)
-        for base in range(0, n_rows, LANES):
-            row = (base + lax.broadcasted_iota(jnp.int32, (LANES, LANES), 0)).astype(i16)
-            count = jnp.zeros((LANES, LANES), bf16)
-            for k in range(fanout):
-                hit = jnp.broadcast_to(where[k : k + 1, :], (LANES, LANES)) == row
-                count += jnp.where(hit, one, zero)
-            counts_ref[rows, base : base + LANES] = count.T
-        mine = nodes[:, j : j + 1]
-        upper = mine >= half
-        chosen = jnp.where(node == jnp.where(upper, mine - half, mine), 1.0, 0.0).astype(bf16)
-        both = jnp.dot(chosen, halves, preferred_element_type=jnp.float32)
-        self_ref[rows, :] = jnp.where(upper, both[:, width:], both[:, :width]).astype(bf16)
+    @pl.when(waits_first())
+    def _():
+        local_work(pick_ref, neighbours_ref, nodes_ref, features_ref, self_ref, counts_ref)
 
 
 def layer_kernel(
     fanout,
     scale,
     arrived_ref,
-    counts_ref,
-    self_ref,
+    early_self_ref,
+    early_counts_ref,
+    features_ref,
+    pick_ref,
+    neighbours_ref,
+    nodes_ref,
     w_self_ref,
     w_neigh_ref,
     cotangent_ref,
     hidden_ref,
     partial_ref,
+    self_ref,
+    counts_ref,
     inputs_ref,
     slope_ref,
 ):
     width = self_ref.shape[1]
     units = cotangent_ref.shape[1]
-    weights = jnp.concatenate([w_self_ref[...], w_neigh_ref[...]], axis=0)
-    total = jnp.dot(counts_ref[...], arrived_ref[...], preferred_element_type=jnp.float32)
-    mean = (total * (1.0 / fanout)).astype(jnp.bfloat16)
-    inputs = jnp.concatenate([self_ref[...], mean], axis=1)
-    inputs_ref[...] = inputs
-    pre = jnp.dot(inputs, weights, preferred_element_type=jnp.float32)
-    sigma = jax.nn.sigmoid(pre)
-    hidden = pre * sigma
-    hidden_ref[...] = hidden.astype(jnp.bfloat16)
-    slope_ref[...] = (
-        cotangent_ref[...].astype(jnp.float32) * (sigma + hidden * (1.0 - sigma))
-    ).astype(jnp.bfloat16)
-    terms = lax.dot_general(
-        inputs_ref[...],
-        slope_ref[...],
-        (((0,), (0,)), ((), ())),
-        preferred_element_type=jnp.float32,
-    )
-    terms = (terms * scale).astype(jnp.bfloat16)
-    for i in range(units // LANES):
-        partial_ref[i * 2 * width : (i + 1) * 2 * width, :] = terms[:, i * LANES : (i + 1) * LANES]
+
+    def layer():
+        weights = jnp.concatenate([w_self_ref[...], w_neigh_ref[...]], axis=0)
+        total = jnp.dot(counts_ref[...], arrived_ref[...], preferred_element_type=jnp.float32)
+        mean = (total * (1.0 / fanout)).astype(jnp.bfloat16)
+        inputs = jnp.concatenate([self_ref[...], mean], axis=1)
+        inputs_ref[...] = inputs
+        pre = jnp.dot(inputs, weights, preferred_element_type=jnp.float32)
+        sigma = jax.nn.sigmoid(pre)
+        hidden = pre * sigma
+        hidden_ref[...] = hidden.astype(jnp.bfloat16)
+        slope_ref[...] = (
+            cotangent_ref[...].astype(jnp.float32) * (sigma + hidden * (1.0 - sigma))
+        ).astype(jnp.bfloat16)
+        terms = lax.dot_general(
+            inputs_ref[...],
+            slope_ref[...],
+            (((0,), (0,)), ((), ())),
+            preferred_element_type=jnp.float32,
+        )
+        terms = (terms * scale).astype(jnp.bfloat16)
+        for i in range(units // LANES):
+            partial_ref[i * 2 * width : (i + 1) * 2 * width, :] = terms[:, i * LANES : (i + 1) * LANES]
+
+    first = waits_first()
+
+    @pl.when(first)
+    def _():
+        layer()
+
+    @pl.when(jnp.logical_not(first))
+    def _():
+        local_work(pick_ref, neighbours_ref, nodes_ref, features_ref, self_ref, counts_ref)
+        layer()
 
 
 def finish_kernel(
@@ -196,34 +234,41 @@
     held = [pltpu.VMEM(x.shape, x.dtype) for x in own]
     outgoing, *held = call(
         serve_kernel,
-        (pltpu.VMEM((n_rows, width), bf16), held[1], held[2], held[3], held[4]),
+        (
+            pltpu.VMEM((n_rows, width), bf16),
+            pltpu.VMEM((batch, width), bf16),
+            pltpu.VMEM((batch, n_rows), bf16),
+            *held[1:],
+        ),
         [pltpu.with_memory_space_constraint(x, pltpu.HBM) for x in own],
-        2 * n_rows * n_nodes * width,
+        2 * (n_rows + batch) * n_nodes * width,
         2 * n_nodes * width,
         (held[0], pltpu.SemaphoreType.DMA((len(own),))),
         [HBM] * len(own),
     )
+    outgoing, w_self, w_neigh, cotangent = lax.optimization_barrier(
+        (outgoing, w_self, w_neigh, cotangent)
+    )
     arrived = lax.all_to_all(
         outgoing.reshape(n_devices, cap, width), SENDS, split_axis=0, concat_axis=0, tiled=True
     ).reshape(n_rows, width)
-    self_rows, counts = call(
-        local_kernel,
-        (struct((batch, width), bf16), struct((batch, n_rows), bf16)),
-        (held[1], held[2], held[3], held[0]),
-        2 * batch * n_nodes * width,
-        2 * n_nodes * width,
-    )
     scale = 1.0 / math.sqrt(n_devices * batch)
-    hidden, partial = call(
+    hidden, partial, _, _ = call(
         functools.partial(layer_kernel, fanout, scale),
         (
             pltpu.VMEM((batch, units), bf16),
             pltpu.VMEM((2 * width * units // LANES, LANES), bf16),
-        ),
-        (arrived, counts, self_rows, w_self, w_neigh, cotangent),
+            pltpu.VMEM((batch, width), bf16),
+            pltpu.VMEM((batch, n_rows), bf16),
+        ),
+        (arrived, *held, w_self, w_neigh, cotangent),
         8 * batch * width * units,
         4 * batch * units,
-        (pltpu.VMEM((batch, 2 * width), bf16), pltpu.VMEM((batch, units), bf16)),
+        (
+            pltpu.VMEM((batch, 2 * width), bf16),
+            pltpu.VMEM((batch, units), bf16),
+        ),
+        aliases={1: 2, 2: 3},
     )
     packed = partial.shape[0]
     share = -(-packed // n_devices)

time: 38.5 us -> 38.3 us (level)
  blocking collectives: 19.3 us -> 32.9 us
  starting transfers between devices: 7.3 us -> 0 us
  waiting for transfers between devices: 5.65 us -> 0 us
  Pallas kernels: 5.19 us -> 4.4 us
    all_to_all x0 -> x1, blocking collectives: none -> 13.3 us  [local(): lax.all_to_all(outgoing.reshape(n_devices, cap, width), SENDS, split_axis...]
    all_to_all x1 -> x0, starting transfers between devices: 7.3 us -> none  [local(): lax.all_to_all(outgoing.reshape(n_devices, cap, width), SENDS, split_axis...]
    all_to_all x1 -> x0, waiting for transfers between devices: 5.65 us -> none  [local(): lax.all_to_all(outgoing.reshape(n_devices, cap, width), SENDS, split_axis...]
    pallas_call x4 -> x3, Pallas kernels: 5.19 us -> 4.4 us  [call(): pl.pallas_call(kernel, out_shape=out_shape, in_specs=places or [VMEM] * l...]
  transfers between devices with their start and end apart: 1 -> 0, of which waited for: 1 -> 0; matrix products, arithmetic and copies ran while one was open for 0% -> 0% of each run, Pallas kernels for 4% -> 0%
where the time goes in v5:
time: 38.3 us; the launch traced here: 38.1 us
  blocking collectives  32.9 us (86%)
  Pallas kernels  4.4 us (11%)
  between operations  0.69 us (2%)
    all_to_all x1, blocking collectives, local(): lax.all_to_all(outgoing.reshape(n_devices, cap, width), SENDS, split_axis...  13.3 us
    all_to_all x1, blocking collectives, local(): lax.all_to_all(jnp.broadcast_to(summed, pieces.shape), SENDS, split_axis=...  10 us
    all_to_all x1, blocking collectives, local(): lax.all_to_all(partial.reshape(n_devices, share, LANES), SENDS, split_axi...  9.63 us
    pallas_call x3, Pallas kernels, call(): pl.pallas_call(kernel, out_shape=out_shape, in_specs=places or [VMEM] * l...  4.4 us

profile of v5, /device:TPU:0, one launch (start us, length us, event | category | flops | bytes accessed | tf_op | source)
XLA Modules:
  0.0 38.1 jit_solution(4072554679800031891)
XLA Ops:
  0.6 0.0 copy-start
  0.6 0.0 copy-start.2
  0.7 2.7 %shard_map.103 = (bf16[128,128]{1,0:T(8,128)(2,1)S(1)}, bf16[1024,128]{1,0:T(8,128)(2,1)S(1)}, bf16[1024,128]{1,0:T(8,128)(2,1)S(1)}, bf16[2048,128]{1,0:T(8,128...) custom-call(s32[4,8]{1,0:T(4,128)} %bitcast.13, bf16[2048,128]{1,0:T(8,128)(2,1)} %features_hbm.1, ...), custom_call_target="tpu_custom_call" | custom-call | flops 603979776 | bytes 524288 | tf_op jit(solution)/shard_map/pallas_call | solution.py:29
  3.3 0.0 copy-start.1
  3.3 13.3 %all_to_all.15 = bf16[32,4,128]{2,1,0:T(4,128)(2,1)S(1)} all-to-all(bf16[32,4,128]{2,1,0:T(4,128)(2,1)S(1)} %bitcast.10), channel_id=1, replica_groups=mesh['dom'=8,'local'=4] {'local','dom'}, dimensions={0} | all-to-all | bytes 65536 | tf_op jit(solution)/shard_map/all_to_all | solution.py:252
  16.6 0.0 copy-done
  16.6 0.0 copy-done.2
  16.6 0.0 copy-done.1
  16.6 0.8 %shard_map.104 = (bf16[1024,256]{1,0:T(8,128)(2,1)S(1)}, bf16[512,128]{1,0:T(8,128)(2,1)S(1)}, bf16[1024,128]{1,0:T(8,128)(2,1)S(1)}, bf16[1024,128]{1,0:T(8,128)(2,1)S(1)}) custom-call(bf16[128,128]{1,0:T(8,128)(2,1)S(1)} %bitcast.8, bf16[1024,128]{1,0:T(8,128)(2,1)S(1)} %get-tuple-element.18.early_self_ref, ...), custom_call_target="tpu_custom_call", output_to_operand_aliasing={{2}: (1, {}), {3}: (2, {})} | custom-call | flops 268435456 | bytes 1048576 | tf_op jit(solution)/shard_map/pallas_call | solution.py:29
  17.5 9.6 %all_to_all.16 = bf16[32,16,128]{2,1,0:T(8,128)(2,1)S(1)} all-to-all(bf16[32,16,128]{2,1,0:T(8,128)(2,1)S(1)} %bitcast.9), channel_id=1, replica_groups=mesh['dom'=8,'local'=4] {'local','dom'}, dimensions={0} | all-to-all | bytes 262144 | tf_op jit(solution)/shard_map/all_to_all | solution.py:277
  27.2 10.0 %all_to_all.17 = bf16[32,16,128]{2,1,0:T(8,128)(2,1)S(1)} all-to-all(bf16[32,16,128]{2,1,0:T(8,128)(2,1)S(1)} %broadcast_in_dim.3), channel_id=1, replica_groups=mesh['dom'=8,'local'=4] {'local','dom'}, dimensions={0} | all-to-all | bytes 262144 | tf_op jit(solution)/shard_map/all_to_all | solution.py:281
  37.2 0.9 %shard_map.105 = (bf16[1024,256]{1,0:T(8,128)(2,1)}, f32[128,256]{1,0:T(8,128)}, f32[128,256]{1,0:T(8,128)}) custom-call(bf16[512,128]{1,0:T(8,128)(2,1)S(1)} %bitcast.7, bf16[1024,256]{1,0:T(8,128)(2,1)S(1)} %get-tuple-element.28.hidden_ref), custom_call_target="tpu_custom_call" | custom-call | bytes 1441792 | tf_op jit(solution)/shard_map/pallas_call | solution.py:29
  (2 shorter events, 0.1 us)
Async XLA Ops:
  0.6 16.0 %copy-start = (bf16[1024,256]{1,0:T(8,128)(2,1)S(1)}, bf16[1024,256]{1,0:T(8,128)(2,1)}, u32[]{:S(2)}) copy-start(bf16[1024,256]{1,0:T(8,128)(2,1)} %cotangent_ref) | copy-start | bytes 1572868
  0.6 16.0 %copy-start.2 = (bf16[128,256]{1,0:T(8,128)(2,1)S(1)}, bf16[128,256]{1,0:T(8,128)(2,1)}, u32[]{:S(2)}) copy-start(bf16[128,256]{1,0:T(8,128)(2,1)} %w_neigh_ref) | copy-start | bytes 196612
  3.3 13.3 %copy-start.1 = (bf16[128,256]{1,0:T(8,128)(2,1)S(1)}, bf16[128,256]{1,0:T(8,128)(2,1)}, u32[]{:S(2)}) copy-start(bf16[128,256]{1,0:T(8,128)(2,1)} %w_self_ref) | copy-start | bytes 196612

commit v6 on v5

--- a/solution.py
+++ b/solution.py
@@ -24,7 +24,6 @@
     scratch=(),
     places=None,
     out=None,
-    aliases={},
 ):
     return pl.pallas_call(
         kernel,
@@ -32,7 +31,6 @@
         in_specs=places or [VMEM] * len(operands),
         out_specs=out or jax.tree.map(lambda _: VMEM, out_shape),
         scratch_shapes=list(scratch),
-        input_output_aliases=aliases,
         compiler_params=pltpu.CompilerParams(vmem_limit_bytes=40 * 2**20),
         cost_estimate=pl.CostEstimate(
             flops=flops, bytes_accessed=bytes_accessed, transcendentals=0
@@ -41,7 +39,7 @@
 
 
 def waits_first():
-    return lax.axis_index("dom") < lax.axis_size("dom") * 6 // 8
+    return lax.axis_index("dom") < lax.axis_size("dom") // 2
 
 
 def local_work(pick_ref, neighbours_ref, nodes_ref, features_ref, self_ref, counts_ref):
@@ -157,15 +155,15 @@
     cotangent_ref,
     hidden_ref,
     partial_ref,
-    self_ref,
-    counts_ref,
+    late_self_ref,
+    late_counts_ref,
     inputs_ref,
     slope_ref,
 ):
-    width = self_ref.shape[1]
+    width = features_ref.shape[1]
     units = cotangent_ref.shape[1]
 
-    def layer():
+    def layer(self_ref, counts_ref):
         weights = jnp.concatenate([w_self_ref[...], w_neigh_ref[...]], axis=0)
         total = jnp.dot(counts_ref[...], arrived_ref[...], preferred_element_type=jnp.float32)
         mean = (total * (1.0 / fanout)).astype(jnp.bfloat16)
@@ -192,12 +190,14 @@
 
     @pl.when(first)
     def _():
-        layer()
+        layer(early_self_ref, early_counts_ref)
 
     @pl.when(jnp.logical_not(first))
     def _():
-        local_work(pick_ref, neighbours_ref, nodes_ref, features_ref, self_ref, counts_ref)
-        layer()
+        local_work(
+            pick_ref, neighbours_ref, nodes_ref, features_ref, late_self_ref, late_counts_ref
+        )
+        layer(late_self_ref, late_counts_ref)
 
 
 def finish_kernel(
@@ -253,22 +253,21 @@
         outgoing.reshape(n_devices, cap, width), SENDS, split_axis=0, concat_axis=0, tiled=True
     ).reshape(n_rows, width)
     scale = 1.0 / math.sqrt(n_devices * batch)
-    hidden, partial, _, _ = call(
+    hidden, partial = call(
         functools.partial(layer_kernel, fanout, scale),
         (
             pltpu.VMEM((batch, units), bf16),
             pltpu.VMEM((2 * width * units // LANES, LANES), bf16),
-            pltpu.VMEM((batch, width), bf16),
-            pltpu.VMEM((batch, n_rows), bf16),
         ),
         (arrived, *held, w_self, w_neigh, cotangent),
         8 * batch * width * units,
         4 * batch * units,
         (
+            pltpu.VMEM((batch, width), bf16),
+            pltpu.VMEM((batch, n_rows), bf16),
             pltpu.VMEM((batch, 2 * width), bf16),
             pltpu.VMEM((batch, units), bf16),
         ),
-        aliases={1: 2, 2: 3},
     )
     packed = partial.shape[0]
     share = -(-packed // n_devices)

time: 38.3 us -> 38.1 us (level)
  no operation moved by 1% of the time
where the time goes in v6:
time: 38.1 us; the launch traced here: 37.9 us
  blocking collectives  32.7 us (86%)
  Pallas kernels  4.4 us (12%)
  between operations  0.69 us (2%)
    all_to_all x1, blocking collectives, local(): lax.all_to_all(outgoing.reshape(n_devices, cap, width), SENDS, split_axis...  13.1 us
    all_to_all x1, blocking collectives, local(): lax.all_to_all(jnp.broadcast_to(summed, pieces.shape), SENDS, split_axis=...  10 us
    all_to_all x1, blocking collectives, local(): lax.all_to_all(partial.reshape(n_devices, share, LANES), SENDS, split_axi...  9.63 us
    pallas_call x3, Pallas kernels, call(): pl.pallas_call(kernel, out_shape=out_shape, in_specs=places or [VMEM] * l...  4.4 us

profile of v6, /device:TPU:0, one launch (start us, length us, event | category | flops | bytes accessed | tf_op | source)
XLA Modules:
  0.0 37.9 jit_solution(4488696208466364758)
XLA Ops:
  0.6 0.0 copy-start
  0.6 0.0 copy-start.2
  0.7 2.7 %shard_map.103 = (bf16[128,128]{1,0:T(8,128)(2,1)S(1)}, bf16[1024,128]{1,0:T(8,128)(2,1)S(1)}, bf16[1024,128]{1,0:T(8,128)(2,1)S(1)}, bf16[2048,128]{1,0:T(8,128...) custom-call(s32[4,8]{1,0:T(4,128)} %bitcast.13, bf16[2048,128]{1,0:T(8,128)(2,1)} %features_hbm.1, ...), custom_call_target="tpu_custom_call" | custom-call | flops 603979776 | bytes 524288 | tf_op jit(solution)/shard_map/pallas_call | solution.py:28
  3.3 0.0 copy-start.1
  3.3 13.1 %all_to_all.15 = bf16[32,4,128]{2,1,0:T(4,128)(2,1)S(1)} all-to-all(bf16[32,4,128]{2,1,0:T(4,128)(2,1)S(1)} %bitcast.10), channel_id=1, replica_groups=mesh['dom'=8,'local'=4] {'local','dom'}, dimensions={0} | all-to-all | bytes 65536 | tf_op jit(solution)/shard_map/all_to_all | solution.py:252
  16.4 0.0 copy-done
  16.4 0.0 copy-done.2
  16.4 0.0 copy-done.1
  16.4 0.8 %shard_map.104 = (bf16[1024,256]{1,0:T(8,128)(2,1)S(1)}, bf16[512,128]{1,0:T(8,128)(2,1)S(1)}) custom-call(bf16[128,128]{1,0:T(8,128)(2,1)S(1)} %bitcast.8, bf16[1024,128]{1,0:T(8,128)(2,1)S(1)} %get-tuple-element.18.early_self_ref, bf16[1024,128]{1,0:T(8,128)(2,1)S(1)} %get-tuple-element.19.early_counts_ref, ...), custom_call_target="tpu_custom_call" | custom-call | flops 268435456 | bytes 1048576 | tf_op jit(solution)/shard_map/pallas_call | solution.py:28
  17.3 9.6 %all_to_all.16 = bf16[32,16,128]{2,1,0:T(8,128)(2,1)S(1)} all-to-all(bf16[32,16,128]{2,1,0:T(8,128)(2,1)S(1)} %bitcast.9), channel_id=1, replica_groups=mesh['dom'=8,'local'=4] {'local','dom'}, dimensions={0} | all-to-all | bytes 262144 | tf_op jit(solution)/shard_map/all_to_all | solution.py:276
  27.0 10.0 %all_to_all.17 = bf16[32,16,128]{2,1,0:T(8,128)(2,1)S(1)} all-to-all(bf16[32,16,128]{2,1,0:T(8,128)(2,1)S(1)} %broadcast_in_dim.3), channel_id=1, replica_groups=mesh['dom'=8,'local'=4] {'local','dom'}, dimensions={0} | all-to-all | bytes 262144 | tf_op jit(solution)/shard_map/all_to_all | solution.py:280
  37.0 0.9 %shard_map.105 = (bf16[1024,256]{1,0:T(8,128)(2,1)}, f32[128,256]{1,0:T(8,128)}, f32[128,256]{1,0:T(8,128)}) custom-call(bf16[512,128]{1,0:T(8,128)(2,1)S(1)} %bitcast.7, bf16[1024,256]{1,0:T(8,128)(2,1)S(1)} %get-tuple-element.28.hidden_ref), custom_call_target="tpu_custom_call" | custom-call | bytes 1441792 | tf_op jit(solution)/shard_map/pallas_call | solution.py:28
  (2 shorter events, 0.1 us)
Async XLA Ops:
  0.6 15.8 %copy-start = (bf16[1024,256]{1,0:T(8,128)(2,1)S(1)}, bf16[1024,256]{1,0:T(8,128)(2,1)}, u32[]{:S(2)}) copy-start(bf16[1024,256]{1,0:T(8,128)(2,1)} %cotangent_ref) | copy-start | bytes 1572868
  0.6 15.8 %copy-start.2 = (bf16[128,256]{1,0:T(8,128)(2,1)S(1)}, bf16[128,256]{1,0:T(8,128)(2,1)}, u32[]{:S(2)}) copy-start(bf16[128,256]{1,0:T(8,128)(2,1)} %w_neigh_ref) | copy-start | bytes 196612
  3.3 13.1 %copy-start.1 = (bf16[128,256]{1,0:T(8,128)(2,1)S(1)}, bf16[128,256]{1,0:T(8,128)(2,1)}, u32[]{:S(2)}) copy-start(bf16[128,256]{1,0:T(8,128)(2,1)} %w_self_ref) | copy-start | bytes 196612

commit v7 on v6

--- a/solution.py
+++ b/solution.py
@@ -103,10 +103,11 @@
     sems,
 ):
     cap, n_dom = serve_ref.shape
-    n_nodes = features_ref.shape[0]
+    n_nodes, width = features_ref.shape
+    half = n_nodes // 2
     pairs = (
+        (features_hbm, features_ref),
         (serve_hbm, serve_ref),
-        (features_hbm, features_ref),
         (pick_hbm, pick_ref),
         (neighbours_hbm, neighbours_ref),
         (nodes_hbm, nodes_ref),
@@ -114,7 +115,7 @@
     fetches = [pltpu.make_async_copy(*pair, sems.at[i]) for i, pair in enumerate(pairs)]
     for fetch in fetches:
         fetch.start()
-    fetches[0].wait()
+    fetches[1].wait()
     serve = serve_ref[...].astype(jnp.float32)
     block = LANES
     picked = []
@@ -126,14 +127,20 @@
         group = lax.broadcasted_iota(jnp.int32, (block, n_dom), 1)
         mine = group == row // cap % n_dom
         index = jnp.sum(jnp.where(mine, wanted, 0.0), axis=1, keepdims=True).astype(jnp.int32)
-        node = lax.broadcasted_iota(jnp.int32, (block, n_nodes), 1)
-        picked.append(jnp.where(node == index, 1.0, 0.0).astype(jnp.bfloat16))
-    for fetch in fetches[1:]:
+        upper = index >= half
+        node = lax.broadcasted_iota(jnp.int32, (block, half), 1)
+        hit = node == jnp.where(upper, index - half, index)
+        picked.append((jnp.where(hit, 1.0, 0.0).astype(jnp.bfloat16), upper))
+    fetches[0].wait()
+    halves = jnp.concatenate([features_ref[:half, :], features_ref[half:, :]], axis=1)
+    for i, (chosen, upper) in enumerate(picked):
+        both = jnp.dot(chosen, halves, preferred_element_type=jnp.float32)
+        out_ref[i * block : (i + 1) * block, :] = jnp.where(
+            upper, both[:, width:], both[:, :width]
+        ).astype(jnp.bfloat16)
+
+    for fetch in fetches[2:]:
         fetch.wait()
-    for i, chosen in enumerate(picked):
-        out_ref[i * block : (i + 1) * block, :] = jnp.dot(
-            chosen, features_ref[...], preferred_element_type=jnp.float32
-        ).astype(jnp.bfloat16)
 
     @pl.when(waits_first())
     def _():
@@ -218,6 +225,14 @@
         copy.wait()
 
 
+def exchange_order(n_dom, n_local):
+    def place(i):
+        dom, local = divmod(i, n_local)
+        return local // 2, dom % 2, (dom // 2) ^ 1, local % 2
+
+    return sorted(range(n_dom * n_local), key=place)
+
+
 def local(features, serve_rows, pick_rows, neighbours, batch_nodes, w_self, w_neigh, cotangent):
     n_dom = lax.axis_size("dom")
     n_local = lax.axis_size("local")
@@ -269,16 +284,22 @@
             pltpu.VMEM((batch, units), bf16),
         ),
     )
+    spread = {
+        "split_axis": 0,
+        "concat_axis": 0,
+        "tiled": True,
+        "axis_index_groups": [exchange_order(n_dom, n_local)],
+    }
     packed = partial.shape[0]
     share = -(-packed // n_devices)
     if share * n_devices != packed:
         partial = jnp.pad(partial, ((0, share * n_devices - packed), (0, 0)))
     pieces = lax.all_to_all(
-        partial.reshape(n_devices, share, LANES), SENDS, split_axis=0, concat_axis=0, tiled=True
+        partial.reshape(n_devices, share, LANES), AXES, **spread
     )
     summed = jnp.sum(pieces.astype(f32), axis=0).astype(bf16)
     gathered = lax.all_to_all(
-        jnp.broadcast_to(summed, pieces.shape), SENDS, split_axis=0, concat_axis=0, tiled=True
+        jnp.broadcast_to(summed, pieces.shape), AXES, **spread
     ).reshape(n_devices * share, LANES)
     grad = struct((width, units), f32)
     return call(

time: 38.1 us -> 37.8 us (level)
  no operation moved by 1% of the time
where the time goes in v7:
time: 37.8 us; the launch traced here: 37.6 us
  blocking collectives  32.5 us (86%)
  Pallas kernels  4.32 us (11%)
  between operations  0.69 us (2%)
    all_to_all x1, blocking collectives, local(): lax.all_to_all(outgoing.reshape(n_devices, cap, width), SENDS, split_axis...  13.1 us
    all_to_all x1, blocking collectives, local(): lax.all_to_all(jnp.broadcast_to(summed, pieces.shape), AXES, **spread)  9.79 us
    all_to_all x1, blocking collectives, local(): lax.all_to_all(partial.reshape(n_devices, share, LANES), AXES, **spread)  9.65 us
    pallas_call x3, Pallas kernels, call(): pl.pallas_call(kernel, out_shape=out_shape, in_specs=places or [VMEM] * l...  4.32 us

profile of v7, /device:TPU:0, one launch (start us, length us, event | category | flops | bytes accessed | tf_op | source)
XLA Modules:
  0.0 37.6 jit_solution(10402916353298265565)
XLA Ops:
  0.6 0.0 copy-start
  0.6 0.0 copy-start.2
  0.7 2.6 %shard_map.103 = (bf16[128,128]{1,0:T(8,128)(2,1)S(1)}, bf16[1024,128]{1,0:T(8,128)(2,1)S(1)}, bf16[1024,128]{1,0:T(8,128)(2,1)S(1)}, bf16[2048,128]{1,0:T(8,128...) custom-call(s32[4,8]{1,0:T(4,128)} %bitcast.13, bf16[2048,128]{1,0:T(8,128)(2,1)} %features_hbm.1, ...), custom_call_target="tpu_custom_call" | custom-call | flops 603979776 | bytes 524288 | tf_op jit(solution)/shard_map/pallas_call | solution.py:28
  3.3 0.0 copy-start.1
  3.3 13.1 %all_to_all.15 = bf16[32,4,128]{2,1,0:T(4,128)(2,1)S(1)} all-to-all(bf16[32,4,128]{2,1,0:T(4,128)(2,1)S(1)} %bitcast.10), channel_id=1, replica_groups=mesh['dom'=8,'local'=4] {'local','dom'}, dimensions={0} | all-to-all | bytes 65536 | tf_op jit(solution)/shard_map/all_to_all | solution.py:267
  16.4 0.0 copy-done
  16.4 0.0 copy-done.2
  16.4 0.0 copy-done.1
  16.4 0.8 %shard_map.104 = (bf16[1024,256]{1,0:T(8,128)(2,1)S(1)}, bf16[512,128]{1,0:T(8,128)(2,1)S(1)}) custom-call(bf16[128,128]{1,0:T(8,128)(2,1)S(1)} %bitcast.8, bf16[1024,128]{1,0:T(8,128)(2,1)S(1)} %get-tuple-element.18.early_self_ref, bf16[1024,128]{1,0:T(8,128)(2,1)S(1)} %get-tuple-element.19.early_counts_ref, ...), custom_call_target="tpu_custom_call" | custom-call | flops 268435456 | bytes 1048576 | tf_op jit(solution)/shard_map/pallas_call | solution.py:28
  17.2 9.6 %all_to_all.16 = bf16[32,16,128]{2,1,0:T(8,128)(2,1)S(1)} all-to-all(bf16[32,16,128]{2,1,0:T(8,128)(2,1)S(1)} %bitcast.9), channel_id=1, replica_groups={{8,9,0,1,24,25,16,17,12,13,4,5,28,29,20,21,10,11,2,3,26,27,18,19,14,15,..., dimensions={0} | all-to-all | bytes 262144 | tf_op jit(solution)/shard_map/all_to_all | solution.py:297
  26.9 9.8 %all_to_all.17 = bf16[32,16,128]{2,1,0:T(8,128)(2,1)S(1)} all-to-all(bf16[32,16,128]{2,1,0:T(8,128)(2,1)S(1)} %broadcast_in_dim.3), channel_id=1, replica_groups={{8,9,0,1,24,25,16,17,12,13,4,5,28,29,20,21,10,11,2,3,26,27,18,19,14,15,..., dimensions={0} | all-to-all | bytes 262144 | tf_op jit(solution)/shard_map/all_to_all | solution.py:301
  36.7 0.9 %shard_map.105 = (bf16[1024,256]{1,0:T(8,128)(2,1)}, f32[128,256]{1,0:T(8,128)}, f32[128,256]{1,0:T(8,128)}) custom-call(bf16[512,128]{1,0:T(8,128)(2,1)S(1)} %bitcast.7, bf16[1024,256]{1,0:T(8,128)(2,1)S(1)} %get-tuple-element.28.hidden_ref), custom_call_target="tpu_custom_call" | custom-call | bytes 1441792 | tf_op jit(solution)/shard_map/pallas_call | solution.py:28
  (2 shorter events, 0.1 us)
Async XLA Ops:
  0.6 15.7 %copy-start = (bf16[1024,256]{1,0:T(8,128)(2,1)S(1)}, bf16[1024,256]{1,0:T(8,128)(2,1)}, u32[]{:S(2)}) copy-start(bf16[1024,256]{1,0:T(8,128)(2,1)} %cotangent_ref) | copy-start | bytes 1572868
  0.6 15.7 %copy-start.2 = (bf16[128,256]{1,0:T(8,128)(2,1)S(1)}, bf16[128,256]{1,0:T(8,128)(2,1)}, u32[]{:S(2)}) copy-start(bf16[128,256]{1,0:T(8,128)(2,1)} %w_neigh_ref) | copy-start | bytes 196612
  3.3 13.1 %copy-start.1 = (bf16[128,256]{1,0:T(8,128)(2,1)S(1)}, bf16[128,256]{1,0:T(8,128)(2,1)}, u32[]{:S(2)}) copy-start(bf16[128,256]{1,0:T(8,128)(2,1)} %w_self_ref) | copy-start | bytes 196612
